TPU v7x, 128 devices: a whole 4x4x4 slice. The times are simulated.
128 devices in a mesh: dp: 16 (over z, x_hi, core), tensor: 8 (over y, x_lo).
Axes of the slice: x: 4 (x_hi: 2, x_lo: 2; x = x_hi * 2 + x_lo), y: 4, z: 4, core: 2. Of those that a mesh axis runs over, the one named last changes fastest.
Arguments:
- tokens: bfloat16 [32768, 1024], P(('dp', 'tensor')), may hold values from -6 to 6
- attn_gain: bfloat16 [1024], replicated, may hold values from 0.099609375 to 1.8984375
- w_query: bfloat16 [1024, 2048], P('dp', 'tensor'), may hold values from -0.1875 to 0.1875
- key_weight: bfloat16 [1024, 1024], P('dp', 'tensor'), may hold values from -0.1875 to 0.1875
- value_weight: bfloat16 [1024, 1024], P('dp', 'tensor'), may hold values from -0.1875 to 0.1875
- query_gain: bfloat16 [128], replicated, may hold values from 0.099609375 to 1.8984375
- key_gain: bfloat16 [128], replicated, may hold values from 0.099609375 to 1.8984375
- w_out: bfloat16 [2048, 1024], P('tensor', 'dp'), may hold values from -0.5 to 0.5
- mlp_gain: bfloat16 [1024], replicated, may hold values from 0.099609375 to 1.8984375
- w_gate: bfloat16 [1024, 3072], P('dp', 'tensor'), may hold values from -0.1875 to 0.1875
- w_up: bfloat16 [1024, 3072], P('dp', 'tensor'), may hold values from -0.1875 to 0.1875
- w_down: bfloat16 [3072, 1024], P('tensor', 'dp'), may hold values from -0.109375 to 0.109375
- out_cotangent: bfloat16 [32768, 1024], P(('dp', 'tensor')), may hold values from -6 to 6
Outputs:
- layer_out: bfloat16 [32768, 1024], P(('dp', 'tensor'))
- input_grad: float32 [32768, 1024], P(('dp', 'tensor'))
- attn_gain_grad: float32 [1024], replicated
- w_query_grad: float32 [1024, 2048], P('dp', 'tensor')
- w_key_grad: float32 [1024, 1024], P('dp', 'tensor')
- w_value_grad: float32 [1024, 1024], P('dp', 'tensor')
- query_gain_grad: float32 [128], replicated
- key_gain_grad: float32 [128], replicated
- w_out_grad: float32 [2048, 1024], P('tensor', 'dp')
- mlp_gain_grad: float32 [1024], replicated
- w_gate_grad: float32 [1024, 3072], P('dp', 'tensor')
- w_up_grad: float32 [1024, 3072], P('dp', 'tensor')
- w_down_grad: float32 [3072, 1024], P('tensor', 'dp')
All inputs are finite; a program needn't handle non-finite values.
Results may differ from a plain program's by a relative error of at most 0.025.
Values may be sent and summed in bfloat16 or wider, within the bound.
A program may use at most 128 MiB of HBM per device.

v0:
```python
import math

import jax
import jax.numpy as jnp
from jax import lax
from jax.sharding import PartitionSpec as P

HEAD_SIZE = 128
SEQUENCE_LENGTH = 1024


eps_norm = 1e-06
rope_base = 1000000.0


def dot_plain(first_op, second_op):
    return jnp.dot(first_op, second_op, preferred_element_type=jnp.float32)


def dot_right_t(first_op, second_op):
    return lax.dot_general(
        first_op, second_op, (((1,), (1,)), ((), ())), preferred_element_type=jnp.float32
    )


def dot_left_t(first_op, second_op):
    return lax.dot_general(
        first_op, second_op, (((0,), (0,)), ((), ())), preferred_element_type=jnp.float32
    )


def rms_scale(values):
    return lax.rsqrt(jnp.mean(values * values, axis=-1, keepdims=True) + eps_norm)


def norm_back(values, inv_scale, gain_vec, grad_out):
    scaled = grad_out * gain_vec
    inner_sum = jnp.mean(scaled * values, axis=-1, keepdims=True)
    return (inv_scale * scaled - values * inv_scale**3 * inner_sum, grad_out * values * inv_scale)


def rope_tables(token_length, head_dim):
    half_dim = head_dim // 2
    position = lax.broadcasted_iota(jnp.float32, (token_length, half_dim), 0)
    channel = lax.broadcasted_iota(jnp.float32, (token_length, half_dim), 1)
    angle_rad = position * jnp.exp(channel * (-2.0 * math.log(rope_base) / head_dim))
    return (jnp.cos(angle_rad)[:, None, :], jnp.sin(angle_rad)[:, None, :])


def rotate(values, cos_table, sin_table):
    half_dim = values.shape[-1] // 2
    first_part = values[..., :half_dim]
    second_part = values[..., half_dim:]
    return jnp.concatenate(
        [
            first_part * cos_table - second_part * sin_table,
            second_part * cos_table + first_part * sin_table,
        ],
        axis=-1,
    )


def rotate_back(grad_vals, cos_table, sin_table):
    half_dim = grad_vals.shape[-1] // 2
    first_part = grad_vals[..., :half_dim]
    second_part = grad_vals[..., half_dim:]
    return jnp.concatenate(
        [
            first_part * cos_table + second_part * sin_table,
            second_part * cos_table - first_part * sin_table,
        ],
        axis=-1,
    )


def causal_mask(start_row, block_rows, stop_row):
    row_pos = lax.broadcasted_iota(jnp.int32, (block_rows, stop_row), 0) + start_row
    col_pos = lax.broadcasted_iota(jnp.int32, (block_rows, stop_row), 1)
    return col_pos <= row_pos


def block_scores(query_block, key_seq, start_row, stop_row):
    score_scale = 1.0 / math.sqrt(HEAD_SIZE)
    scores = (
        jnp.einsum(
            "bkgd,jkd->kgbj", query_block, key_seq[:stop_row], preferred_element_type=jnp.float32
        )
        * score_scale
    )
    return jnp.where(causal_mask(start_row, stop_row - start_row, stop_row), scores, -1e30)


def attend_forward(operands):
    query_sequence, key_seq, value_seq = operands
    token_length = query_sequence.shape[0]
    kv_heads = key_seq.shape[1]
    grouped_heads = query_sequence.reshape(
        token_length, kv_heads, query_sequence.shape[1] // kv_heads, HEAD_SIZE
    )
    block_rows = min(512, token_length)
    outputs = []
    totals = []
    for block_index in range(token_length // block_rows):
        start_row = block_index * block_rows
        stop_row = start_row + block_rows
        scores = block_scores(grouped_heads[start_row:stop_row], key_seq, start_row, stop_row)
        top_score = jnp.max(scores, axis=-1, keepdims=True)
        exp_scores = jnp.exp(scores - top_score)
        total_sum = jnp.sum(exp_scores, axis=-1, keepdims=True)
        prob_low = (exp_scores / total_sum).astype(jnp.bfloat16)
        outputs.append(
            jnp.einsum(
                "kgbj,jkd->bkgd", prob_low, value_seq[:stop_row], preferred_element_type=jnp.float32
            )
        )
        totals.append(top_score[..., 0] + jnp.log(total_sum[..., 0]))
    return (jnp.concatenate(outputs, axis=0), jnp.concatenate(totals, axis=2))


def attend_backward(operands):
    query_sequence, key_seq, value_seq, grad_seq, log_total = operands
    token_length = query_sequence.shape[0]
    kv_heads = key_seq.shape[1]
    group_size = query_sequence.shape[1] // kv_heads
    grouped_heads = query_sequence.reshape(token_length, kv_heads, group_size, HEAD_SIZE)
    grad_grouped = grad_seq.reshape(token_length, kv_heads, group_size, HEAD_SIZE)
    score_scale = 1.0 / math.sqrt(HEAD_SIZE)
    block_rows = min(512, token_length)
    key_grad = jnp.zeros(key_seq.shape, jnp.float32)
    value_grad = jnp.zeros(value_seq.shape, jnp.float32)
    query_grads = []
    for block_index in range(token_length // block_rows):
        start_row = block_index * block_rows
        stop_row = start_row + block_rows
        query_block = grouped_heads[start_row:stop_row]
        grad_block = grad_grouped[start_row:stop_row]
        scores = block_scores(query_block, key_seq, start_row, stop_row)
        prob_rows = jnp.exp(scores - log_total[:, :, start_row:stop_row, None])
        prob_low = prob_rows.astype(jnp.bfloat16)
        grad_probs = jnp.einsum(
            "bkgd,jkd->kgbj", grad_block, value_seq[:stop_row], preferred_element_type=jnp.float32
        )
        row_inner = jnp.sum(prob_rows * grad_probs, axis=-1, keepdims=True)
        grad_scores = (prob_rows * (grad_probs - row_inner)).astype(jnp.bfloat16)
        query_grads.append(
            jnp.einsum(
                "kgbj,jkd->bkgd",
                grad_scores,
                key_seq[:stop_row],
                preferred_element_type=jnp.float32,
            )
            * score_scale
        )
        key_grad = key_grad.at[:stop_row].add(
            jnp.einsum(
                "kgbj,bkgd->jkd", grad_scores, query_block, preferred_element_type=jnp.float32
            )
            * score_scale
        )
        value_grad = value_grad.at[:stop_row].add(
            jnp.einsum("kgbj,bkgd->jkd", prob_low, grad_block, preferred_element_type=jnp.float32)
        )
    query_grad = jnp.concatenate(query_grads, axis=0).reshape(
        token_length, kv_heads * group_size, HEAD_SIZE
    )
    return (query_grad, key_grad, value_grad)


def rows_gather(rows_part):
    return lax.all_gather(rows_part, "tensor", axis=0, tiled=True)


def rows_sum(partial_rows):
    return lax.psum_scatter(
        partial_rows.astype(jnp.bfloat16), "tensor", scatter_dimension=0, tiled=True
    ).astype(jnp.float32)


def project_rows(split_low, weight_rows):
    return rows_sum(dot_plain(split_low, weight_rows))


def fetch_attention(w_query, key_weight, value_weight):
    return (
        lax.all_gather(w_query, "dp", axis=0, tiled=True),
        lax.all_gather(key_weight, "dp", axis=0, tiled=True),
        lax.all_gather(value_weight, "dp", axis=0, tiled=True),
    )


def fetch_mlp(w_gate, w_up):
    return (
        lax.all_gather(w_gate, "dp", axis=0, tiled=True),
        lax.all_gather(w_up, "dp", axis=0, tiled=True),
    )


def fetch_output(w_part):
    return lax.all_gather(w_part, "dp", axis=1, tiled=True)


def return_output(grad_part):
    return lax.psum_scatter(
        grad_part.astype(jnp.bfloat16), "dp", scatter_dimension=1, tiled=True
    ).astype(jnp.float32)


def body(
    tokens,
    attn_gain,
    w_query,
    key_weight,
    value_weight,
    query_gain,
    key_gain,
    w_out,
    mlp_gain,
    w_gate,
    w_up,
    w_down,
    out_cotangent,
):
    rows_x = tokens.astype(jnp.float32)
    attn_gain_f = attn_gain.astype(jnp.float32)
    mlp_gain_f = mlp_gain.astype(jnp.float32)
    query_gain_f = query_gain.astype(jnp.float32)
    key_gain_f = key_gain.astype(jnp.float32)
    cos_table, sin_table = rope_tables(SEQUENCE_LENGTH, HEAD_SIZE)
    inv_attn = rms_scale(rows_x)
    attn_full = rows_gather((rows_x * inv_attn * attn_gain_f).astype(jnp.bfloat16))
    group_rows = attn_full.shape[0]
    sequence_count = group_rows // SEQUENCE_LENGTH
    query_w, key_w, value_w = fetch_attention(w_query, key_weight, value_weight)
    out_w = fetch_output(w_out)
    query_pre = dot_plain(attn_full, query_w).reshape(
        sequence_count, SEQUENCE_LENGTH, -1, HEAD_SIZE
    )
    key_before_norm = dot_plain(attn_full, key_w).reshape(
        sequence_count, SEQUENCE_LENGTH, -1, HEAD_SIZE
    )
    value_low = (
        dot_plain(attn_full, value_w)
        .astype(jnp.bfloat16)
        .reshape(sequence_count, SEQUENCE_LENGTH, -1, HEAD_SIZE)
    )
    query_inv = rms_scale(query_pre)
    key_inv = rms_scale(key_before_norm)
    query_low = rotate(query_pre * query_inv * query_gain_f, cos_table, sin_table).astype(
        jnp.bfloat16
    )
    key_low = rotate(key_before_norm * key_inv * key_gain_f, cos_table, sin_table).astype(
        jnp.bfloat16
    )
    mixed_rows, log_total = lax.map(attend_forward, (query_low, key_low, value_low))
    mixed_low = mixed_rows.reshape(group_rows, -1).astype(jnp.bfloat16)
    resid = rows_x + project_rows(mixed_low, out_w)
    inv_mlp = rms_scale(resid)
    mlp_full = rows_gather((resid * inv_mlp * mlp_gain_f).astype(jnp.bfloat16))
    gate_w, up_w = fetch_mlp(w_gate, w_up)
    down_w = fetch_output(w_down)
    gate_pre = dot_plain(mlp_full, gate_w)
    up_pre = dot_plain(mlp_full, up_w)
    gate_sig = jax.nn.sigmoid(gate_pre)
    gate_act = gate_pre * gate_sig
    hidden_low = (gate_act * up_pre).astype(jnp.bfloat16)
    layer_out = (resid + project_rows(hidden_low, down_w)).astype(jnp.bfloat16)
    back_down_w = fetch_output(w_down)
    back_gate_w, back_up_w = fetch_mlp(w_gate, w_up)
    back_out_w = fetch_output(w_out)
    back_query_w, back_key_w, back_value_w = fetch_attention(w_query, key_weight, value_weight)
    cot_full = rows_gather(out_cotangent)
    w_down_grad = return_output(dot_left_t(hidden_low, cot_full))
    hidden_grad = dot_right_t(cot_full, back_down_w)
    gate_grad_low = (hidden_grad * up_pre * gate_sig * (1.0 + gate_pre * (1.0 - gate_sig))).astype(
        jnp.bfloat16
    )
    up_grad_low = (hidden_grad * gate_act).astype(jnp.bfloat16)
    mlp_rows_grad = rows_sum(
        dot_right_t(gate_grad_low, back_gate_w) + dot_right_t(up_grad_low, back_up_w)
    )
    w_gate_grad, w_up_grad = (
        lax.psum_scatter(
            dot_left_t(mlp_full, gate_grad_low).astype(jnp.bfloat16),
            "dp",
            scatter_dimension=0,
            tiled=True,
        ).astype(jnp.float32),
        lax.psum_scatter(
            dot_left_t(mlp_full, up_grad_low).astype(jnp.bfloat16),
            "dp",
            scatter_dimension=0,
            tiled=True,
        ).astype(jnp.float32),
    )
    resid_from, mlp_gain_part = norm_back(resid, inv_mlp, mlp_gain_f, mlp_rows_grad)
    resid_grad = out_cotangent.astype(jnp.float32) + resid_from
    resid_grad_full = rows_gather(resid_grad.astype(jnp.bfloat16))
    w_out_grad = return_output(dot_left_t(mixed_low, resid_grad_full))
    mixed_grad = (
        dot_right_t(resid_grad_full, back_out_w)
        .astype(jnp.bfloat16)
        .reshape(sequence_count, SEQUENCE_LENGTH, -1, HEAD_SIZE)
    )
    query_grad, key_grad, value_grad = lax.map(
        attend_backward, (query_low, key_low, value_low, mixed_grad, log_total)
    )
    query_pre_grad, query_gain_part = norm_back(
        query_pre, query_inv, query_gain_f, rotate_back(query_grad, cos_table, sin_table)
    )
    key_pre_grad, key_gain_part = norm_back(
        key_before_norm, key_inv, key_gain_f, rotate_back(key_grad, cos_table, sin_table)
    )
    query_pre_low = query_pre_grad.reshape(group_rows, -1).astype(jnp.bfloat16)
    key_pre_low = key_pre_grad.reshape(group_rows, -1).astype(jnp.bfloat16)
    value_pre_low = value_grad.reshape(group_rows, -1).astype(jnp.bfloat16)
    attn_rows_grad = rows_sum(
        dot_right_t(query_pre_low, back_query_w)
        + dot_right_t(key_pre_low, back_key_w)
        + dot_right_t(value_pre_low, back_value_w)
    )
    w_query_grad, w_key_grad, w_value_grad = (
        lax.psum_scatter(
            dot_left_t(attn_full, query_pre_low).astype(jnp.bfloat16),
            "dp",
            scatter_dimension=0,
            tiled=True,
        ).astype(jnp.float32),
        lax.psum_scatter(
            dot_left_t(attn_full, key_pre_low).astype(jnp.bfloat16),
            "dp",
            scatter_dimension=0,
            tiled=True,
        ).astype(jnp.float32),
        lax.psum_scatter(
            dot_left_t(attn_full, value_pre_low).astype(jnp.bfloat16),
            "dp",
            scatter_dimension=0,
            tiled=True,
        ).astype(jnp.float32),
    )
    input_from, attn_gain_part = norm_back(rows_x, inv_attn, attn_gain_f, attn_rows_grad)
    input_grad = resid_grad + input_from
    attn_gain_grad, mlp_gain_grad, query_gain_grad, key_gain_grad = lax.psum(
        (
            jnp.sum(attn_gain_part, axis=0),
            jnp.sum(mlp_gain_part, axis=0),
            jnp.sum(query_gain_part, axis=(0, 1, 2)),
            jnp.sum(key_gain_part, axis=(0, 1, 2)),
        ),
        ("dp", "tensor"),
    )
    return (
        layer_out,
        input_grad,
        attn_gain_grad,
        w_query_grad,
        w_key_grad,
        w_value_grad,
        query_gain_grad,
        key_gain_grad,
        w_out_grad,
        mlp_gain_grad,
        w_gate_grad,
        w_up_grad,
        w_down_grad,
    )


def solution(mesh):
    return jax.shard_map(
        body,
        mesh=mesh,
        in_specs=(
            P(("dp", "tensor"), None),
            P(),
            P("dp", "tensor"),
            P("dp", "tensor"),
            P("dp", "tensor"),
            P(),
            P(),
            P("tensor", "dp"),
            P(),
            P("dp", "tensor"),
            P("dp", "tensor"),
            P("tensor", "dp"),
            P(("dp", "tensor"), None),
        ),
        out_specs=(
            P(("dp", "tensor"), None),
            P(("dp", "tensor"), None),
            P(),
            P("dp", "tensor"),
            P("dp", "tensor"),
            P("dp", "tensor"),
            P(),
            P(),
            P("tensor", "dp"),
            P(),
            P("dp", "tensor"),
            P("dp", "tensor"),
            P("tensor", "dp"),
        ),
        check_vma=False,
    )
```

profile of v0, /device:TPU:8, one launch (start us, length us, event | category | flops | bytes accessed | tf_op | source)
XLA Modules:
  0.0 1349.0 jit_solution(15916031269045093622)
XLA Ops:
  9.8 2.0 fusion.95
  13.2 27.9 %all_gather.42 = bf16[1024,128]{1,0:T(8,128)(2,1)S(1)} all-gather(bf16[64,128]{1,0:T(8,128)(2,1)} %param.32), channel_id=1, replica_groups=mesh['dp'=16,'tensor'=8] {'dp'}, dimensions={0}, use_global_device_ids=true | all-gather | bytes 278528 | tf_op jit(solution)/shard_map/all_gather | solution.py:186
  41.1 22.7 %all_gather.41 = bf16[1024,128]{1,0:T(8,128)(2,1)S(1)} all-gather(bf16[64,128]{1,0:T(8,128)(2,1)} %param.33), channel_id=1, replica_groups=mesh['dp'=16,'tensor'=8] {'dp'}, dimensions={0}, use_global_device_ids=true | all-gather | bytes 278528 | tf_op jit(solution)/shard_map/all_gather | solution.py:187
  64.8 29.6 %all_gather.43 = bf16[1024,256]{1,0:T(8,128)(2,1)S(1)} all-gather(bf16[64,256]{1,0:T(8,128)(2,1)S(1)} %copy-done.54), channel_id=1, replica_groups=mesh['dp'=16,'tensor'=8] {'dp'}, dimensions={0}, use_global_device_ids=true | all-gather | bytes 557056 | tf_op jit(solution)/shard_map/all_gather | solution.py:185
  94.4 27.7 %all_gather.44 = bf16[256,1024]{0,1:T(8,128)(2,1)} all-gather(bf16[256,64]{0,1:T(8,128)(2,1)S(1)} %copy-done.55), channel_id=1, replica_groups=mesh['dp'=16,'tensor'=8] {'dp'}, dimensions={1}, use_global_device_ids=true | all-gather | bytes 557056 | tf_op jit(solution)/shard_map/all_gather | solution.py:199
  122.1 4.8 fusion.108
  126.9 2.3 reshape.721
  129.2 3.2 multiply_reduce_fusion.1
  132.5 2.4 copy.201
  134.9 3.5 multiply_reduce_fusion.5
  145.9 4.3 convolution_convert_fusion.3
  150.2 15.4 %while.35 = (s32[]{:T(128)}, bf16[2,1024,1,2,128]{1,4,3,2,0:T(8,128)(2,1)}, f32[2,1,2,1024]{3,2,1,0:T(2,128)S(1)}, bf16[2,1024,1,128]{3,1,0,2:T(8,128)(2,1)}, bf...) while((s32[]{:T(128)}, ...), condition=%wide.region_8.9_spmd, body=%wide.region_3.8_spmd.sunk | while | flops 823919104 | bytes 33905332 | solution.py:254
  165.5 2.4 copy.205
  168.0 4.7 convolution_convert_fusion.1
  173.4 88.1 %reduce-scatter.12.cloned.1.call-done = bf16[256,1024]{1,0:T(8,128)(2,1)} async-done(((bf16[2048,1024]{1,0:T(8,128)(2,1)}), bf16[256,1024]{1,0:T(8,128)(2,1)}) %reduce-scatter.12.cloned.1.call-update) | async-done | bytes 524304 | tf_op jit(solution)/shard_map/reduce_scatter | solution.py:174
  262.8 2.0 multiply_convert_fusion.3
  265.5 33.1 %all_gather.46 = bf16[1024,384]{1,0:T(8,128)(2,1)} all-gather(bf16[64,384]{1,0:T(8,128)(2,1)S(1)} %copy-done.50), channel_id=1, replica_groups=mesh['dp'=16,'tensor'=8] {'dp'}, dimensions={0}, use_global_device_ids=true | all-gather | bytes 835584 | tf_op jit(solution)/shard_map/all_gather | solution.py:193
  298.5 30.4 %all_gather.47 = bf16[1024,384]{1,0:T(8,128)(2,1)S(1)} all-gather(bf16[64,384]{1,0:T(8,128)(2,1)S(1)} %copy-done.51), channel_id=1, replica_groups=mesh['dp'=16,'tensor'=8] {'dp'}, dimensions={0}, use_global_device_ids=true | all-gather | bytes 835584 | tf_op jit(solution)/shard_map/all_gather | solution.py:194
  329.0 35.0 %all_gather.48 = bf16[384,1024]{0,1:T(8,128)(2,1)} all-gather(bf16[384,64]{0,1:T(8,128)(2,1)S(1)} %copy-done.52), channel_id=1, replica_groups=mesh['dp'=16,'tensor'=8] {'dp'}, dimensions={1}, use_global_device_ids=true | all-gather | bytes 835584 | tf_op jit(solution)/shard_map/all_gather | solution.py:199
  364.0 10.8 all-gather.7.cloned.1.call-done
  374.7 6.4 fusion.110
  381.2 4.1 fusion.109
  385.3 81.7 %all-gather.9.cloned.1.call-done = bf16[2048,1024]{1,0:T(8,128)(2,1)} async-done(((bf16[256,1024]{1,0:T(8,128)(2,1)}), bf16[2048,1024]{1,0:T(8,128)(2,1)}) %all-gather.9.cloned.1.call-update) | async-done | bytes 4194320 | tf_op jit(solution)/shard_map/all_gather | solution.py:170
  467.0 9.2 multiply_convert_fusion
  476.2 2.4 fusion.111
  478.6 4.6 add_convert_fusion.1
  483.7 90.9 %reduce-scatter.16.cloned.1.call-done = bf16[256,1024]{1,0:T(8,128)(2,1)} async-done(((bf16[2048,1024]{1,0:T(8,128)(2,1)}), bf16[256,1024]{1,0:T(8,128)(2,1)}) %reduce-scatter.16.cloned.1.call-update) | async-done | bytes 524304 | tf_op jit(solution)/shard_map/reduce_scatter | solution.py:174
  576.0 2.3 fusion.106
  578.3 6.0 convolution_convert_fusion.4
  584.4 5.9 convolution_convert_fusion.5
  593.2 6.0 convolution_convert_fusion.6
  599.4 69.7 %all-gather.11.cloned.1.call-done = bf16[2048,1024]{1,0:T(8,128)(2,1)} async-done(((bf16[256,1024]{1,0:T(8,128)(2,1)}), bf16[2048,1024]{1,0:T(8,128)(2,1)}) %all-gather.11.cloned.1.call-update) | async-done | bytes 4194320 | tf_op jit(solution)/shard_map/all_gather | solution.py:170
  669.1 4.4 convolution_convert_fusion.2
  673.6 2.1 reshape.722
  675.7 48.7 %while.36 = (s32[]{:T(128)}, f32[2,1024,2,128]{1,3,2,0:T(8,128)}, f32[2,1024,1,128]{1,3,2,0:T(8,128)}, bf16[2,1024,1,128]{3,1,0,2:T(8,128)(2,1)}, bf16[2,1024,1,...) while((s32[]{:T(128)}, f32[2,1024,2,128]{1,3,2,0:T(8,128)}, ...), condition=%wide.region_17.18_spmd, body=%wide.region_14.17_spmd.sunk | while | flops 2035612160 | bytes 120004968 | solution.py:304
  685.1 2.1 fusion.219
  690.7 4.0 fusion.209
  709.3 2.1 fusion.219
  715.0 4.0 fusion.209
  726.5 2.7 multiply_add_fusion
  730.9 4.3 convolution_convert_fusion.9
  735.2 2.2 multiply_reduce_fusion.2
  738.8 4.5 fusion.112
  743.4 3.4 pad_maximum_fusion
  746.9 4.2 copy.211
  752.4 4.3 convolution_convert_fusion.10
  756.8 4.9 convolution_convert_fusion.7
  761.8 2.8 mul.708
  764.7 2.6 mul.669.clone
  767.3 2.6 mul.713
  771.0 4.5 fusion.113
  775.5 2.1 convolution_convert_fusion.8
  777.7 9.1 add_convert_fusion
  787.9 5.8 convolution_convert_fusion
  795.3 14.2 %reduce-scatter.30.cloned.1.call-done = bf16[64,384]{1,0:T(8,128)(2,1)} async-done(((bf16[1024,384]{1,0:T(8,128)(2,1)}), bf16[64,384]{1,0:T(8,128)(2,1)}) %reduce-scatter.30.cloned.1.call-update) | async-done | bytes 49168 | tf_op jit(solution)/shard_map/reduce_scatter | solution.py:288
  811.0 67.5 %reduce-scatter.28.cloned.1.call-done = bf16[64,384]{1,0:T(8,128)(2,1)} async-done(((bf16[1024,384]{1,0:T(8,128)(2,1)}), bf16[64,384]{1,0:T(8,128)(2,1)}) %reduce-scatter.28.cloned.1.call-update) | async-done | bytes 49168 | tf_op jit(solution)/shard_map/reduce_scatter | solution.py:282
  880.0 66.7 %reduce-scatter.24.cloned.1.call-done = bf16[64,128]{1,0:T(8,128)(2,1)} async-done(((bf16[1024,128]{1,0:T(8,128)(2,1)}), bf16[64,128]{1,0:T(8,128)(2,1)}) %reduce-scatter.24.cloned.1.call-update) | async-done | bytes 16400 | tf_op jit(solution)/shard_map/reduce_scatter | solution.py:334
  948.0 67.0 %reduce-scatter.22.cloned.1.call-done = bf16[64,128]{1,0:T(8,128)(2,1)} async-done(((bf16[1024,128]{1,0:T(8,128)(2,1)}), bf16[64,128]{1,0:T(8,128)(2,1)}) %reduce-scatter.22.cloned.1.call-update) | async-done | bytes 16400 | tf_op jit(solution)/shard_map/reduce_scatter | solution.py:328
  1016.4 67.3 %reduce-scatter.26.cloned.1.call-done = bf16[256,64]{0,1:T(8,128)(2,1)} async-done(((bf16[256,1024]{0,1:T(8,128)(2,1)}), bf16[256,64]{0,1:T(8,128)(2,1)}) %reduce-scatter.26.cloned.1.call-update) | async-done | bytes 32784 | tf_op jit(solution)/shard_map/reduce_scatter | solution.py:203
  1085.1 67.5 %reduce-scatter.20.cloned.1.call-done = bf16[64,256]{1,0:T(8,128)(2,1)} async-done(((bf16[1024,256]{1,0:T(8,128)(2,1)}), bf16[64,256]{1,0:T(8,128)(2,1)}) %reduce-scatter.20.cloned.1.call-update) | async-done | bytes 32784 | tf_op jit(solution)/shard_map/reduce_scatter | solution.py:322
  1153.9 90.3 %reduce-scatter.18.cloned.1.call-done = bf16[256,1024]{1,0:T(8,128)(2,1)} async-done(((bf16[2048,1024]{1,0:T(8,128)(2,1)}), bf16[256,1024]{1,0:T(8,128)(2,1)}) %reduce-scatter.18.cloned.1.call-update) | async-done | bytes 524304 | tf_op jit(solution)/shard_map/reduce_scatter | solution.py:174
  1245.6 67.3 %all-reduce.2 = (f32[1024]{0:T(1024)}, f32[128]{0:T(128)}, f32[128]{0:T(128)}, f32[1024]{0:T(1024)}) all-reduce(f32[1024]{0:T(1024)S(1)} %get-tuple-element.361, f32[128]{0:T(128)S(1)} %bitcast_reduce_fusion, f32[128]{0:T(128)S(1)} %get-tuple-element.357, ...), channel_id=1, replica_groups=mesh['dp'=16,'tensor'=8] {'dp','tensor'}, use_global_device_ids=true, to_apply=%region_23.24 | all-reduce | flops 2304 | bytes 18432 | tf_op jit(solution)/shard_map/psum | solution.py:343
  1312.9 26.1 %reduce-scatter.14.cloned.1.call-done = bf16[256,1024]{1,0:T(8,128)(2,1)} async-done(((bf16[2048,1024]{1,0:T(8,128)(2,1)}), bf16[256,1024]{1,0:T(8,128)(2,1)}) %reduce-scatter.14.cloned.1.call-update) | async-done | bytes 524304 | tf_op jit(solution)/shard_map/reduce_scatter | solution.py:174
  1339.0 3.0 fusion.87
  (295 shorter events, 91.2 us)
Async XLA Ops:
  7.2 57.6 %copy-start.54 = (bf16[64,256]{1,0:T(8,128)(2,1)S(1)}, bf16[64,256]{1,0:T(8,128)(2,1)}, u32[]{:S(2)}) copy-start(bf16[64,256]{1,0:T(8,128)(2,1)} %param.31) | copy-start | bytes 98308
  7.2 87.2 %copy-start.55 = (bf16[256,64]{0,1:T(8,128)(2,1)S(1)}, bf16[256,64]{0,1:T(8,128)(2,1)}, u32[]{:S(2)}) copy-start(bf16[256,64]{0,1:T(8,128)(2,1)} %param.36) | copy-start | bytes 98308
  7.2 114.9 %all-gather.5.cloned.1.call-start = ((), (), s32[]{:S(2)}) async-start(), calls=%async_computation.11 | async-start | bytes 4718592 | tf_op jit(solution)/shard_map/all_gather | solution.py:170
  9.1 54.7 %copy-start.56 = (f32[256]{0:T(256)}, f32[256]{0:T(256)S(1)}, u32[]{:S(2)}) copy-start(f32[256]{0:T(256)S(1)} %get-tuple-element.433) | copy-start | bytes 3076
  9.8 54.0 %copy-start.48 = (f32[1024]{0:T(1024)}, f32[1024]{0:T(1024)S(1)}, u32[]{:S(2)}) copy-start(f32[1024]{0:T(1024)S(1)} %convert_element_type.174) | copy-start | bytes 12292
  11.8 249.7 %reduce-scatter.12.cloned.1.call-start = ((), (), s32[]{:S(2)}) async-start(), calls=%async_computation.12 | async-start | bytes 4718592 | tf_op jit(solution)/shard_map/reduce_scatter | solution.py:174
  13.2 127.2 %copy-start.58 = (f32[128]{0:T(128)}, f32[128]{0:T(128)S(1)}, u32[]{:S(2)}) copy-start(f32[128]{0:T(128)S(1)} %convert_element_type.177) | copy-start | bytes 1540
  41.1 93.8 %copy-start.28 = (bf16[1024,128]{1,0:T(8,128)(2,1)}, bf16[1024,128]{1,0:T(8,128)(2,1)S(1)}, u32[]{:S(2)}) copy-start(bf16[1024,128]{1,0:T(8,128)(2,1)S(1)} %all_gather.42) | copy-start | bytes 786436
  63.8 82.1 %copy-start.39 = (bf16[1024,128]{1,0:T(8,128)(2,1)}, bf16[1024,128]{1,0:T(8,128)(2,1)S(1)}, u32[]{:S(2)}) copy-start(bf16[1024,128]{1,0:T(8,128)(2,1)S(1)} %all_gather.41) | copy-start | bytes 786436
  64.8 80.0 %copy-start.13 = (f32[1024,64]{0,1:T(8,128)}, f32[1024,64]{0,1:T(8,128)S(1)}, u32[]{:S(2)}) copy-start(f32[1024,64]{0,1:T(8,128)S(1)} %get-tuple-element.436) | copy-start | bytes 786436
  64.8 80.0 %copy-start.14 = (f32[1024,64]{0,1:T(8,128)}, f32[1024,64]{0,1:T(8,128)S(1)}, u32[]{:S(2)}) copy-start(f32[1024,64]{0,1:T(8,128)S(1)} %get-tuple-element.437) | copy-start | bytes 786436
  94.4 27.7 %copy-start.30 = (bf16[1024,256]{1,0:T(8,128)(2,1)}, bf16[1024,256]{1,0:T(8,128)(2,1)S(1)}, u32[]{:S(2)}) copy-start(bf16[1024,256]{1,0:T(8,128)(2,1)S(1)} %all_gather.43) | copy-start | bytes 1572868
  138.4 3.7 copy-start.4
  139.1 2.8 copy-start.46
  168.0 4.7 copy-start.11
  172.7 88.8 %copy-start.2 = (bf16[256,1024]{1,0:T(8,128)(2,1)S(1)}, bf16[256,1024]{1,0:T(8,128)(2,1)}, u32[]{:S(2)}) copy-start(bf16[256,1024]{1,0:T(8,128)(2,1)} %param.29) | copy-start | bytes 1572868
  172.7 92.8 %copy-start.50 = (bf16[64,384]{1,0:T(8,128)(2,1)S(1)}, bf16[64,384]{1,0:T(8,128)(2,1)}, u32[]{:S(2)}) copy-start(bf16[64,384]{1,0:T(8,128)(2,1)} %param.38) | copy-start | bytes 147460
  172.7 125.8 %copy-start.51 = (bf16[64,384]{1,0:T(8,128)(2,1)S(1)}, bf16[64,384]{1,0:T(8,128)(2,1)}, u32[]{:S(2)}) copy-start(bf16[64,384]{1,0:T(8,128)(2,1)} %param.39) | copy-start | bytes 147460
  172.7 156.2 %copy-start.52 = (bf16[384,64]{0,1:T(8,128)(2,1)S(1)}, bf16[384,64]{0,1:T(8,128)(2,1)}, u32[]{:S(2)}) copy-start(bf16[384,64]{0,1:T(8,128)(2,1)} %param.40) | copy-start | bytes 147460
  172.8 202.0 %all-gather.7.cloned.1.call-start = ((), (), s32[]{:S(2)}) async-start(), calls=%async_computation.13 | async-start | bytes 4718592 | tf_op jit(solution)/shard_map/all_gather | solution.py:170
  264.9 202.1 %all-gather.9.cloned.1.call-start = ((), (), s32[]{:S(2)}) async-start(), calls=%async_computation.15 | async-start | bytes 4718592 | tf_op jit(solution)/shard_map/all_gather | solution.py:170
  265.4 309.1 %reduce-scatter.16.cloned.1.call-start = ((), (), s32[]{:S(2)}) async-start(), calls=%async_computation.16 | async-start | bytes 4718592 | tf_op jit(solution)/shard_map/reduce_scatter | solution.py:174
  374.7 6.5 copy-start.25
  374.7 6.5 copy-start.62
  467.0 9.2 copy-start.26
  476.2 2.4 copy-start.27
  476.2 2.4 copy-start.36
  483.2 91.4 %copy-start.6 = (bf16[256,1024]{1,0:T(8,128)(2,1)S(1)}, bf16[256,1024]{1,0:T(8,128)(2,1)}, u32[]{:S(2)}) copy-start(bf16[256,1024]{1,0:T(8,128)(2,1)} %reduce-scatter.12.cloned.1.call-done) | copy-start | bytes 1572868
  483.2 92.8 %copy-start.16 = (bf16[256,1024]{1,0:T(8,128)(2,1)S(1)}, bf16[256,1024]{1,0:T(8,128)(2,1)}, u32[]{:S(2)}) copy-start(bf16[256,1024]{1,0:T(8,128)(2,1)} %param.41) | copy-start | bytes 1572868
  483.2 185.9 %all-gather.11.cloned.1.call-start = ((), (), s32[]{:S(2)}) async-start(), calls=%async_computation.17 | async-start | bytes 4718592 | tf_op jit(solution)/shard_map/all_gather | solution.py:170
  578.3 215.5 %reduce-scatter.32.cloned.1.call-start = ((), (), s32[]{:S(2)}) async-start(), calls=%async_computation.25 | async-start | bytes 835584 | tf_op jit(solution)/shard_map/reduce_scatter | solution.py:203
  584.3 225.3 %reduce-scatter.30.cloned.1.call-start = ((), (), s32[]{:S(2)}) async-start(), calls=%async_computation.24 | async-start | bytes 835584 | tf_op jit(solution)/shard_map/reduce_scatter | solution.py:288
  590.3 288.2 %reduce-scatter.28.cloned.1.call-start = ((), (), s32[]{:S(2)}) async-start(), calls=%async_computation.23 | async-start | bytes 835584 | tf_op jit(solution)/shard_map/reduce_scatter | solution.py:282
  593.2 76.0 %copy-start.32 = (bf16[256,1024]{0,1:T(8,128)(2,1)S(1)}, bf16[256,1024]{0,1:T(8,128)(2,1)}, u32[]{:S(2)}) copy-start(bf16[256,1024]{0,1:T(8,128)(2,1)} %all_gather.44) | copy-start | bytes 1572868
  599.2 347.5 %reduce-scatter.24.cloned.1.call-start = ((), (), s32[]{:S(2)}) async-start(), calls=%async_computation.21 | async-start | bytes 278528 | tf_op jit(solution)/shard_map/reduce_scatter | solution.py:334
  690.7 4.0 copy-start.1
  715.0 4.0 copy-start.1
  726.5 4.4 copy-start.37
  730.9 4.3 copy-start.5
  730.9 4.3 copy-start.47
  730.9 4.3 copy-start.59
  730.9 6.6 copy-start.53
  735.2 2.3 copy-start.8
  735.2 3.5 copy-start.29
  738.8 4.6 copy-start.23
  738.8 4.6 copy-start.24
  743.3 271.7 %reduce-scatter.22.cloned.1.call-start = ((), (), s32[]{:S(2)}) async-start(), calls=%async_computation.20 | async-start | bytes 278528 | tf_op jit(solution)/shard_map/reduce_scatter | solution.py:328
  752.4 4.4 copy-start.12
  756.7 5.0 copy-start.20
  756.7 326.9 %reduce-scatter.26.cloned.1.call-start = ((), (), s32[]{:S(2)}) async-start(), calls=%async_computation.22 | async-start | bytes 557056 | tf_op jit(solution)/shard_map/reduce_scatter | solution.py:203
  761.7 2.9 copy-start.19
  761.7 390.8 %reduce-scatter.20.cloned.1.call-start = ((), (), s32[]{:S(2)}) async-start(), calls=%async_computation.19 | async-start | bytes 557056 | tf_op jit(solution)/shard_map/reduce_scatter | solution.py:322
  761.8 5.5 copy-start.21
  764.6 5.2 copy-start.9
  764.6 5.2 copy-start.10
  771.0 4.5 copy-start.15
  777.6 466.5 %reduce-scatter.18.cloned.1.call-start = ((), (), s32[]{:S(2)}) async-start(), calls=%async_computation.18 | async-start | bytes 4718592 | tf_op jit(solution)/shard_map/reduce_scatter | solution.py:174
  786.8 552.2 %reduce-scatter.14.cloned.1.call-start = ((), (), s32[]{:S(2)}) async-start(), calls=%async_computation.14 | async-start | bytes 4718592 | tf_op jit(solution)/shard_map/reduce_scatter | solution.py:174
  793.7 450.5 %copy-start.49 = (f32[1024]{0:T(1024)S(1)}, f32[1024]{0:T(1024)}, u32[]{:S(2)}) copy-start(f32[1024]{0:T(1024)} %copy-done.48) | copy-start | bytes 12292
  793.7 450.5 %copy-start.57 = (f32[256]{0:T(256)S(1)}, f32[256]{0:T(256)}, u32[]{:S(2)}) copy-start(f32[256]{0:T(256)} %copy-done.56) | copy-start | bytes 3076
  793.7 545.3 %copy-start.7 = (bf16[256,1024]{1,0:T(8,128)(2,1)S(1)}, bf16[256,1024]{1,0:T(8,128)(2,1)}, u32[]{:S(2)}) copy-start(bf16[256,1024]{1,0:T(8,128)(2,1)} %reduce-scatter.12.cloned.1.call-done) | copy-start | bytes 1572868
  793.7 545.3 %copy-start.17 = (bf16[256,1024]{1,0:T(8,128)(2,1)S(1)}, bf16[256,1024]{1,0:T(8,128)(2,1)}, u32[]{:S(2)}) copy-start(bf16[256,1024]{1,0:T(8,128)(2,1)} %param.41) | copy-start | bytes 1572868
  793.7 545.3 %copy-start.18 = (bf16[256,1024]{1,0:T(8,128)(2,1)S(1)}, bf16[256,1024]{1,0:T(8,128)(2,1)}, u32[]{:S(2)}) copy-start(bf16[256,1024]{1,0:T(8,128)(2,1)} %reduce-scatter.16.cloned.1.call-done) | copy-start | bytes 1572868
  793.7 545.3 %copy-start.60 = (f32[256]{0:T(256)S(1)}, f32[256]{0:T(256)}, u32[]{:S(2)}) copy-start(f32[256]{0:T(256)} %get-tuple-element.432) | copy-start | bytes 3076
  (23 other events, 34.4 us)
Sparse Core Ops, SparseCore 0:
  11.9 105.3 all-gather.4
  172.8 88.5 reduce-scatter.11
  265.0 109.7 all-gather.6
  376.2 90.7 all-gather.8
  483.3 91.1 reduce-scatter.15
  578.4 90.6 all-gather.10
  672.9 67.1 reduce-scatter.31
  744.5 65.0 reduce-scatter.29
  813.4 65.0 reduce-scatter.27
  882.5 64.1 reduce-scatter.23
  950.8 64.2 reduce-scatter.21
  1019.1 64.5 reduce-scatter.25
  1087.9 64.5 reduce-scatter.19
  1154.9 89.2 reduce-scatter.17
  1246.6 92.3 reduce-scatter.13
where the time goes:
time: 1360 us; the launch traced here: 1350 us
  waiting for transfers between devices  809 us (59%)
  blocking collectives  274 us (20%)
  matrix products  138 us (10%)
  other arithmetic  57.1 us (4%)
  local copies, waits for them, and re-layouts  54.8 us (4%)
  between operations  15 us (1%)
    reduce_scatter x4, waiting for transfers between devices, rows_sum(): lax.psum_scatter(partial_rows.astype(jnp.bfloat16), 'tensor', scatter_dim...  295 us
    all_gather x4, waiting for transfers between devices, rows_gather(): return lax.all_gather(rows_part, 'tensor', axis=0, tiled=True)  162 us
    reduce_scatter x1, waiting for transfers between devices, body(): lax.psum_scatter(dot_left_t(mlp_full, gate_grad_low).astype(jnp.bfloat16)...  67.5 us
    reduce_scatter x1, waiting for transfers between devices, body(): lax.psum_scatter(dot_left_t(attn_full, query_pre_low).astype(jnp.bfloat16...  67.5 us
    reduce_scatter x2, waiting for transfers between devices, return_output(): lax.psum_scatter(grad_part.astype(jnp.bfloat16), 'dp', scatter_dimension=...  67.3 us
    psum x1, blocking collectives, body(): lax.psum((jnp.sum(attn_gain_part, axis=0), jnp.sum(mlp_gain_part, axis=0)...  67.3 us
    reduce_scatter x1, waiting for transfers between devices, body(): lax.psum_scatter(dot_left_t(attn_full, key_pre_low).astype(jnp.bfloat16),...  67 us
    reduce_scatter x1, waiting for transfers between devices, body(): lax.psum_scatter(dot_left_t(attn_full, value_pre_low).astype(jnp.bfloat16...  66.7 us
  transfers between devices with their start and end apart: 15, of which 13 were waited for; matrix products, arithmetic and copies ran while one was open for 12% of the time, Pallas kernels for 0%

commit v1 on v0

v1 whole, which is shorter than its diff:
```python
import math

import jax
import jax.numpy as jnp
import numpy as np
from jax import lax
from jax.experimental import pallas as pl
from jax.experimental.pallas import tpu as pltpu
from jax.sharding import PartitionSpec as P

HEAD = 128
SEQ = 1024
WIDTH = 1024
ROWS = 256
QKV = 512
AW = 768
HID = 384
MW = 3 * HID
EPS = 1e-06
ROPE_BASE = 1000000.0
EXP_SCALE = math.log2(math.e) / math.sqrt(HEAD)
SCORE_SCALE = 1.0 / math.sqrt(HEAD)
MESH = pl.DeviceIdType.MESH
F32 = jnp.float32
BF16 = jnp.bfloat16


def dot_nn(a, b):
    return jnp.dot(a, b, preferred_element_type=F32)


def dot_nt(a, b):
    return lax.dot_general(a, b, (((1,), (1,)), ((), ())), preferred_element_type=F32)


def dot_tn(a, b):
    return lax.dot_general(a, b, (((0,), (0,)), ((), ())), preferred_element_type=F32)


def reorder(v):
    return jnp.concatenate([v[:, :512], v[:, 768:], v[:, 512:768]], axis=1)


def row_scale(v):
    return lax.rsqrt(jnp.mean(v * v, axis=-1, keepdims=True) + EPS)


def flip(bit):
    return 1 - bit


SCRATCH = {
    "w_attn": ((2, 2, 2, 2, 2, 64, AW), BF16),
    "w_mlp": ((2, 2, 2, 2, 2, 64, MW), BF16),
    "a_full": ((4, ROWS, WIDTH), BF16),
    "m_full": ((4, ROWS, WIDTH), BF16),
    "c_full": ((4, ROWS, WIDTH), BF16),
    "d_full": ((4, ROWS, WIDTH), BF16),
    "qkp": ((2, 4, ROWS, 384), F32),
    "qs": ((2, 4, 512, HEAD), BF16),
    "ks": ((2, 4, ROWS, HEAD), BF16),
    "kt": ((2, 4, HEAD, ROWS), BF16),
    "vs": ((2, 4, ROWS, HEAD), BF16),
    "vt": ((2, 4, HEAD, ROWS), BF16),
    "os": ((2, 4, 512, HEAD), BF16),
    "linv": ((2, 4, 8, 512), F32),
    "delta": ((2, 4, 8, 512), F32),
    "dos": ((2, 4, 512, HEAD), BF16),
    "dk": ((2, 4, ROWS, HEAD), F32),
    "dv": ((2, 4, ROWS, HEAD), F32),
    "hid": ((2, 4, ROWS, HID), BF16),
    "dgu": ((2, 4, ROWS, 2 * HID), BF16),
    "own": ((ROWS, WIDTH), F32),
    "own_down": ((ROWS, WIDTH), F32),
    "resid": ((ROWS, WIDTH), F32),
    "stage": ((3, ROWS, WIDTH), BF16),
    "stage_down": ((3, ROWS, WIDTH), BF16),
    "rs_q_d": ((2, 128, WIDTH), BF16),
    "rs_q_n": ((2, ROWS, WIDTH), BF16),
    "rs_m": ((3, ROWS, WIDTH), BF16),
    "rs_d": ((3, ROWS, WIDTH), BF16),
    "gains": ((8, WIDTH), F32),
    "gain_in": ((7, 8, WIDTH), F32),
    "core_in": ((2, 2, 2, 2, 1, 64, AW), BF16),
    "mlp_x": ((2, 64, MW), BF16),
    "mlp_c": ((64, MW), F32),
    "attn_x": ((64, AW), F32),
    "attn_sum": ((64, AW), F32),
    "mlp_sum": ((2, 64, MW), F32),
}
AXES = {"xo": 3, "yo": 0, "za": 2, "zb": 1}
ORDER = ["xo", "yo", "za", "zb"]


def part_axes(part):
    return [ORDER[(part + step) % 4] for step in range(4)]


def cube_shape(part, step, cores, width):
    shape = [1, 1, 1, 1]
    for axis in part_axes(part)[:step]:
        shape[AXES[axis]] = 2
    return (*shape, cores, 16, width)


for _part in range(4):
    for _step in range(4):
        SCRATCH[f"ra_{_part}_{_step}"] = (cube_shape(_part, _step, 1, AW), BF16)
        SCRATCH[f"rm_{_part}_{_step}"] = (cube_shape(_part, _step, 2, MW), BF16)

NAMES = list(SCRATCH)
N_SEM = 200
INPUTS = ["tok", "cot", "pa", "pm", "ag", "mg", "qg", "kg", "cosf", "sinf"]
OUTPUTS = ["layer_out", "input_grad", "d_attn", "d_mlp", "d_gain"]


class Refs:
    pass


def kernel(*refs):
    r = Refs()
    names = INPUTS + OUTPUTS + NAMES
    for name, ref in zip(names, refs):
        setattr(r, name, ref)
    ssem, rsem = refs[len(names)], refs[len(names) + 1]

    dp = lax.axis_index("dp")
    tn = lax.axis_index("tensor")
    z = dp // 4
    x_hi = (dp // 2) % 2
    core = dp % 2
    y = tn // 2
    x_lo = tn % 2
    y_lo = y % 2
    y_hi = y // 2
    gz = jnp.where(z < 2, z, 5 - z)
    own_bit = {"xo": x_hi, "yo": y_hi, "za": gz % 2, "zb": gz // 2}
    nbr = {
        "c": (dp + 1 - 2 * core, tn),
        "x": (dp, tn + 1 - 2 * x_lo),
        "y": (dp, tn + 2 - 4 * y_lo),
        "xo": (dp + 2 - 4 * x_hi, tn + 1 - 2 * x_lo),
        "yo": (dp, (3 - y) * 2 + x_lo),
        "za": (dp + 4 - 8 * (z % 2), tn),
        "zb": (dp + 4 * (3 - 2 * z), tn),
    }
    b_own = y_lo * 2 + x_lo
    b_x = y_lo * 2 + flip(x_lo)
    b_y = flip(y_lo) * 2 + x_lo
    b_d = flip(y_lo) * 2 + flip(x_lo)
    i_own = y_lo * 2 + core
    i_c = y_lo * 2 + flip(core)
    i_y = flip(y_lo) * 2 + core
    i_yc = flip(y_lo) * 2 + flip(core)

    counter = [0]
    unsent = []

    def rcopy(src, dst, to):
        i = counter[0]
        counter[0] += 1
        return pltpu.make_async_remote_copy(
            src_ref=src,
            dst_ref=dst,
            send_sem=ssem.at[i],
            recv_sem=rsem.at[i],
            device_id=nbr[to],
            device_id_type=MESH,
        )

    def send(src, dst, to):
        copy = rcopy(src, dst, to)
        copy.start()
        unsent.append(copy)
        return copy

    def flush():
        while unsent:
            unsent.pop().wait_send()

    def own_slot(cores):
        return (
            pl.ds(own_bit["yo"], 1),
            pl.ds(own_bit["zb"], 1),
            pl.ds(own_bit["za"], 1),
            pl.ds(own_bit["xo"], 1),
            cores,
        )

    def slots(full, current, cores):
        index = [None] * 4
        for axis in ORDER:
            if axis in full:
                index[AXES[axis]] = pl.ds(0, 2)
            else:
                bit = own_bit[axis]
                if current is not None and current == axis:
                    bit = flip(bit)
                index[AXES[axis]] = pl.ds(bit, 1)
        return (*index, cores)

    both = pl.ds(0, 2)
    lane = pl.ds(core, 1)

    def gather_step(w, step, cores):
        copies = []
        for part in range(4):
            axes = part_axes(part)
            rows = pl.ds(16 * part, 16)
            view = w.at[(*slots(axes[:step], None, cores), rows)]
            copies.append(send(view, view, axes[step]))
        return copies

    def wait_recv(copies):
        for copy in copies:
            copy.wait_recv()

    def core_send(w, late):
        copies = []
        for part in range(4):
            axes = part_axes(part)
            rows = pl.ds(16 * part, 16)
            current = axes[3] if late else None
            view = w.at[(*slots(axes[:3], current, lane), rows)]
            copies.append(send(view, view, "c"))
        return copies

    def reduce_send(w, bufs, step, cores):
        copies = []
        for part in range(4):
            axes = part_axes(part)
            rows = pl.ds(16 * part, 16)
            view = w.at[(*slots(axes[:step], axes[step], cores), rows)]
            copies.append(send(view, getattr(r, f"{bufs}_{part}_{step}"), axes[step]))
        return copies

    def reduce_add(w, bufs, step, cores, copies):
        for part in range(4):
            axes = part_axes(part)
            rows = pl.ds(16 * part, 16)
            index = (*slots(axes[:step], None, cores), rows)
            copies[part].wait_recv()
            total = w[index].astype(F32) + getattr(r, f"{bufs}_{part}_{step}")[...].astype(F32)
            w[index] = total.astype(BF16)

    barrier = pltpu.get_barrier_semaphore()
    for to in nbr:
        pl.semaphore_signal(barrier, inc=1, device_id=nbr[to], device_id_type=MESH)
    pl.semaphore_wait(barrier, len(nbr))

    swap = rcopy(r.pa, r.w_attn.at[(own_bit["yo"], own_bit["zb"], own_bit["za"], own_bit["xo"], core)], "x")
    mlp_own = r.w_mlp.at[(own_bit["yo"], own_bit["zb"], own_bit["za"], own_bit["xo"], core)]
    mlp_pair = r.w_mlp.at[(own_bit["yo"], own_bit["zb"], own_bit["za"], own_bit["xo"])]
    mlp_to_core = rcopy(r.pm, mlp_own, "c")
    mlp_to_x = rcopy(mlp_pair, mlp_pair, "x")
    carries = core == x_lo
    lends = core != x_lo

    @pl.when(x_hi == 1)
    def _():
        swap.start()

    @pl.when(lends)
    def _():
        mlp_to_core.start()

    @pl.when(x_hi == 0)
    def _():
        r.w_attn[own_slot(lane)] = r.pa[...].reshape(1, 1, 1, 1, 1, 64, AW)

    @pl.when(carries)
    def _():
        r.w_mlp[own_slot(lane)] = r.pm[...].reshape(1, 1, 1, 1, 1, 64, MW)

    attn_gain = reorder(r.ag[...].astype(F32))
    mlp_gain = reorder(r.mg[...].astype(F32))
    query_gain = r.qg[...].astype(F32)
    key_gain = r.kg[...].astype(F32)
    rows_x = reorder(r.tok[...].astype(F32))
    r.a_full[b_own] = (rows_x * row_scale(rows_x) * attn_gain).astype(BF16)

    def square_gather(buf):
        def half(block, n):
            return buf.at[block, pl.ds(128 * n, 128)]

        x0 = send(half(b_own, 0), half(b_own, 0), "x")
        y1 = send(half(b_own, 1), half(b_own, 1), "y")
        x1 = send(half(b_own, 1), half(b_own, 1), "x")
        y0 = send(half(b_own, 0), half(b_own, 0), "y")

        def forward():
            x0.wait_recv()
            fy = send(half(b_x, 0), half(b_x, 0), "y")
            y1.wait_recv()
            fx = send(half(b_y, 1), half(b_y, 1), "x")
            return [x1, y0, fx, fy]

        return forward

    a_forward = square_gather(r.a_full)

    @pl.when(x_hi == 1)
    def _():
        swap.wait_recv()

    step_a = gather_step(r.w_attn, 0, lane)

    @pl.when(carries)
    def _():
        mlp_to_core.wait_recv()
        mlp_to_x.start()

    r.c_full[i_own] = reorder(r.cot[...])
    c_core = send(r.c_full.at[i_own], r.c_full.at[i_own], "c")
    c_y = send(r.c_full.at[i_own], r.c_full.at[i_own], "y")

    wait_recv(step_a)
    step_a = gather_step(r.w_attn, 1, lane)
    a_rest = a_forward()
    wait_recv(step_a)
    step_a = gather_step(r.w_attn, 2, lane)

    @pl.when(lends)
    def _():
        mlp_to_x.wait_recv()

    wait_recv(step_a)
    step_a = gather_step(r.w_attn, 3, lane)
    early = core_send(r.w_attn, False)
    step_m = gather_step(r.w_mlp, 0, both)
    wait_recv(step_a)
    late = core_send(r.w_attn, True)
    wait_recv(a_rest)
    wait_recv(early)
    wait_recv(late)
    wait_recv(step_m)
    step_m = gather_step(r.w_mlp, 1, both)

    def w_qkv(g):
        return r.w_attn[g, :, :, :, :, :, 0:QKV].reshape(WIDTH, QKV)

    def w_o(g):
        return r.w_attn[g, :, :, :, :, :, QKV:AW].reshape(WIDTH, 256)

    def w_gu(g):
        return r.w_mlp[g, :, :, :, :, :, 0 : 2 * HID].reshape(WIDTH, 2 * HID)

    def w_dn(g):
        return r.w_mlp[g, :, :, :, :, :, 2 * HID : MW].reshape(WIDTH, HID)

    def qkv_block(blk, carry):
        rows = r.a_full[blk]
        cos = r.cosf[blk]
        sin = r.sinf[blk]
        for g in range(2):
            acc = dot_nn(rows, w_qkv(g))
            r.qkp[g, blk] = acc[:, :384]
            for h in range(3):
                pre = acc[:, h * HEAD : (h + 1) * HEAD]
                normed = pre * row_scale(pre) * (key_gain if h == 2 else query_gain)
                turned = normed * cos + pltpu.roll(normed, 64, 1) * sin
                if h == 2:
                    r.ks[g, blk] = turned.astype(BF16)
                    r.kt[g, blk] = turned.T.astype(BF16)
                else:
                    r.qs[g, blk, h * ROWS : (h + 1) * ROWS] = turned.astype(BF16)
            value = acc[:, 384:]
            r.vs[g, blk] = value.astype(BF16)
            r.vt[g, blk] = value.T.astype(BF16)
        return carry

    lax.fori_loop(0, 4, qkv_block, 0)
    wait_recv(step_m)
    step_m = gather_step(r.w_mlp, 2, both)

    key_at = lax.broadcasted_iota(jnp.int32, (ROWS, 512), 0)
    query_at = lax.broadcasted_iota(jnp.int32, (ROWS, 512), 1) % ROWS
    visible = key_at <= query_at

    def weights_t(g, i, j, diagonal):
        scores = dot_nt(r.ks[g, j], r.qs[g, i])
        exps = jnp.exp2(scores * EXP_SCALE)
        if diagonal:
            exps = jnp.where(visible, exps, 0.0)
        return exps

    def attend_step(i, j, carry, diagonal):
        out = []
        for g in range(2):
            total, acc = carry[g]
            exps = weights_t(g, i, j, diagonal)
            total = total + jnp.sum(exps, axis=0, keepdims=True)
            acc = acc + dot_nn(r.vt[g, j], exps.astype(BF16))
            out.append((total, acc))
        return tuple(out)

    def attend_block(i, carry):
        zero = (jnp.zeros((1, 512), F32), jnp.zeros((HEAD, 512), F32))
        state = lax.fori_loop(0, i, lambda j, s: attend_step(i, j, s, False), (zero, zero))
        state = attend_step(i, i, state, True)
        for g in range(2):
            total, acc = state[g]
            inv = 1.0 / total
            r.linv[g, i] = jnp.broadcast_to(inv, (8, 512))
            mixed = acc * inv
            r.os[g, i] = mixed.T.astype(BF16)
        return carry

    lax.fori_loop(0, 4, attend_block, 0)
    wait_recv(step_m)
    step_m = gather_step(r.w_mlp, 3, both)

    def square_sum(part_of, near, far, finish_own):
        flush()
        r.stage[2] = part_of(b_d).astype(BF16)
        d0 = send(r.stage.at[2, pl.ds(0, 128)], far.at[0], "x")
        d1 = send(r.stage.at[2, pl.ds(128, 128)], far.at[1], "y")
        r.stage[0] = part_of(b_x).astype(BF16)
        x0 = send(r.stage.at[0, pl.ds(0, 128)], near.at[0, pl.ds(0, 128)], "x")
        r.stage[1] = part_of(b_y).astype(BF16)
        y1 = send(r.stage.at[1, pl.ds(128, 128)], near.at[1, pl.ds(128, 128)], "y")
        d1.wait_recv()
        r.stage[0, 128:256] = (r.stage[0, 128:256].astype(F32) + far[1].astype(F32)).astype(BF16)
        x1 = send(r.stage.at[0, pl.ds(128, 128)], near.at[0, pl.ds(128, 128)], "x")
        d0.wait_recv()
        r.stage[1, 0:128] = (r.stage[1, 0:128].astype(F32) + far[0].astype(F32)).astype(BF16)
        y0 = send(r.stage.at[1, pl.ds(0, 128)], near.at[1, pl.ds(0, 128)], "y")
        r.own[...] = part_of(b_own)
        finish_own()
        wait_recv([x0, y1, x1, y0])
        return r.own[...] + near[0].astype(F32) + near[1].astype(F32)

    def part_o(blk):
        acc = jnp.zeros((ROWS, WIDTH), F32)
        for g in range(2):
            heads = r.os[g, blk]
            acc = acc + dot_nt(jnp.concatenate([heads[:ROWS], heads[ROWS:]], axis=1), w_o(g))
        return acc

    def forward_cot():
        c_y.wait_recv()
        forwards.append(send(r.c_full.at[i_y], r.c_full.at[i_y], "c"))

    forwards = []
    resid = rows_x_again(r) + square_sum(part_o, r.rs_q_n, r.rs_q_d, forward_cot)
    r.resid[...] = resid

    r.m_full[i_own] = (resid * row_scale(resid) * mlp_gain).astype(BF16)
    m_core = send(r.m_full.at[i_own], r.m_full.at[i_own], "c")
    m_y = []
    for n in range(2):
        view = r.m_full.at[i_own, pl.ds(128 * n, 128)]
        m_y.append(send(view, view, "y"))
    wait_recv(step_m)
    c_core.wait_recv()
    wait_recv(forwards)

    def mlp_block(i):
        rows = r.m_full[i]
        cots = r.c_full[i]
        for g in range(2):
            pre = dot_nn(rows, w_gu(g))
            grad = dot_nn(cots, w_dn(g))
            gate = pre[:, :HID]
            up = pre[:, HID:]
            sig = 1.0 / (1.0 + jnp.exp(-gate))
            act = gate * sig
            r.hid[g, i] = (act * up).astype(BF16)
            r.dgu[g, i, :, 0:HID] = (grad * up * sig * (1.0 + gate * (1.0 - sig))).astype(BF16)
            r.dgu[g, i, :, HID : 2 * HID] = (grad * act).astype(BF16)

    mlp_block(i_own)
    m_core.wait_recv()
    mlp_block(i_c)
    m_f = []
    for n in range(2):
        view = r.m_full.at[i_y, pl.ds(128 * n, 128)]
        m_y[n].wait_recv()
        m_f.append(send(view, view, "c"))
    mlp_block(i_y)
    wait_recv(m_f)
    mlp_block(i_yc)

    def pair_sum(part_of, stage, recv, own):
        stage[2] = part_of(i_yc).astype(BF16)
        s3 = send(stage.at[2], recv.at[0], "c")
        stage[0] = part_of(i_c).astype(BF16)
        s1 = send(stage.at[0], recv.at[1], "c")
        near = part_of(i_y)
        s3.wait_recv()
        stage[1] = (near + recv[0].astype(F32)).astype(BF16)
        s2 = send(stage.at[1], recv.at[2], "y")
        own[...] = part_of(i_own)

        def finish():
            wait_recv([s1, s2])
            return own[...] + recv[1].astype(F32) + recv[2].astype(F32)

        return finish

    def part_dm(i):
        return dot_nt(r.dgu[0, i], w_gu(0)) + dot_nt(r.dgu[1, i], w_gu(1))

    def part_down(i):
        return dot_nt(r.hid[0, i], w_dn(0)) + dot_nt(r.hid[1, i], w_dn(1))

    flush()
    dm_finish = pair_sum(part_dm, r.stage, r.rs_m, r.own)
    down_finish = pair_sum(part_down, r.stage_down, r.rs_d, r.own_down)
    r.own_down[...] += r.resid[...]

    @pl.when(carries)
    def _():
        mlp_to_x.wait_send()

    for p in range(4):
        cols = pl.ds(256 * p, 256)
        rows_t = r.m_full[:, :, cols].reshape(SEQ, 256)
        cots_t = r.c_full[:, :, cols].reshape(SEQ, 256)
        for g in range(2):
            grad_gu = dot_tn(rows_t, r.dgu[g].reshape(SEQ, 2 * HID))
            grad_dn = dot_tn(cots_t, r.hid[g].reshape(SEQ, HID))
            r.w_mlp[g, p // 2, p % 2, :, :, :, 0 : 2 * HID] = grad_gu.reshape(2, 2, 64, 2 * HID).astype(BF16)
            r.w_mlp[g, p // 2, p % 2, :, :, :, 2 * HID : MW] = grad_dn.reshape(2, 2, 64, HID).astype(BF16)
    step_m = reduce_send(r.w_mlp, "rm", 3, both)

    dm = dm_finish()
    resid = r.resid[...]
    inv_m = row_scale(resid)
    scaled = dm * mlp_gain
    inner = jnp.mean(scaled * resid, axis=-1, keepdims=True)
    r.gains[...] = jnp.zeros((8, WIDTH), F32)
    r.gains[1:2] = jnp.sum(dm * resid * inv_m, axis=0, keepdims=True)
    dresid = reorder(r.cot[...].astype(F32)) + inv_m * scaled - resid * (inv_m * inv_m * inv_m * inner)
    r.resid[...] = dresid
    r.d_full[b_own] = dresid.astype(BF16)
    d_forward = square_gather(r.d_full)

    down = down_finish()
    r.layer_out[...] = reorder(down).astype(BF16)
    d_rest = d_forward()
    reduce_add(r.w_mlp, "rm", 3, both, step_m)
    step_m = reduce_send(r.w_mlp, "rm", 2, both)
    wait_recv(d_rest)

    def do_block(blk, carry):
        rows = r.d_full[blk]
        for g in range(2):
            grad = dot_nn(rows, w_o(g))
            for h in range(2):
                part = grad[:, h * HEAD : (h + 1) * HEAD].astype(BF16)
                r.dos[g, blk, h * ROWS : (h + 1) * ROWS] = part
                prod = part.astype(F32) * r.os[g, blk, h * ROWS : (h + 1) * ROWS].astype(F32)
                inner = jnp.sum(prod.T, axis=0, keepdims=True)
                r.delta[g, blk, :, h * ROWS : (h + 1) * ROWS] = jnp.broadcast_to(inner, (8, ROWS))
            r.dk[g, blk] = jnp.zeros((ROWS, HEAD), F32)
            r.dv[g, blk] = jnp.zeros((ROWS, HEAD), F32)
        return carry

    lax.fori_loop(0, 4, do_block, 0)
    reduce_add(r.w_mlp, "rm", 2, both, step_m)
    step_m = reduce_send(r.w_mlp, "rm", 1, both)

    def back_step(i, j, carry, diagonal):
        out = []
        for g in range(2):
            probs = weights_t(g, i, j, diagonal) * r.linv[g, i, 0:1]
            grads = dot_nt(r.vs[g, j], r.dos[g, i])
            dz = (probs * (grads - r.delta[g, i, 0:1])).astype(BF16)
            r.dv[g, j] += dot_nn(probs.astype(BF16), r.dos[g, i])
            r.dk[g, j] += dot_nn(dz, r.qs[g, i])
            out.append(carry[g] + dot_nn(r.kt[g, j], dz))
        return tuple(out)

    def unnorm(pre, gain, grad):
        inv = row_scale(pre)
        hat = pre * inv
        scaled = grad * gain
        back = inv * (scaled - hat * jnp.mean(scaled * hat, axis=-1, keepdims=True))
        return back.astype(BF16), jnp.sum(grad * hat, axis=0, keepdims=True)

    def turn_back(grad, blk):
        return grad * r.cosf[blk] - pltpu.roll(grad, 64, 1) * r.sinf[blk]

    def back_block(i, gain_sum):
        zero = jnp.zeros((HEAD, 512), F32)
        state = lax.fori_loop(0, i, lambda j, s: back_step(i, j, s, False), (zero, zero))
        state = back_step(i, i, state, True)
        for g in range(2):
            for h in range(2):
                grad = turn_back(state[g][:, h * ROWS : (h + 1) * ROWS].T * SCORE_SCALE, i)
                low, part = unnorm(r.qkp[g, i, :, h * HEAD : (h + 1) * HEAD], query_gain, grad)
                r.dgu[g, i, :, h * HEAD : (h + 1) * HEAD] = low
                gain_sum = gain_sum + part
        return gain_sum

    q_gain_part = lax.fori_loop(0, 4, back_block, jnp.zeros((1, HEAD), F32))

    def key_block(j, gain_sum):
        for g in range(2):
            grad = turn_back(r.dk[g, j] * SCORE_SCALE, j)
            low, part = unnorm(r.qkp[g, j, :, 256:384], key_gain, grad)
            r.dgu[g, j, :, 256:384] = low
            r.dgu[g, j, :, 384:512] = r.dv[g, j].astype(BF16)
            gain_sum = gain_sum + part
        return gain_sum

    k_gain_part = lax.fori_loop(0, 4, key_block, jnp.zeros((1, HEAD), F32))
    r.gains[2:3, 0:HEAD] = q_gain_part
    r.gains[2:3, HEAD : 2 * HEAD] = k_gain_part
    reduce_add(r.w_mlp, "rm", 1, both, step_m)
    step_m = reduce_send(r.w_mlp, "rm", 0, both)

    def part_da(blk):
        acc = dot_nt(r.dgu[0, blk, :, 0:QKV], w_qkv(0)) + dot_nt(r.dgu[1, blk, :, 0:QKV], w_qkv(1))
        r.gains[0:1] += jnp.sum(acc * r.a_full[blk].astype(F32), axis=0, keepdims=True)
        return acc

    tail = {}

    def attn_grads():
        reduce_add(r.w_mlp, "rm", 0, both, step_m)

        @pl.when(lends)
        def _():
            mlp_back_x.start()

        for p in range(4):
            cols = pl.ds(256 * p, 256)
            rows_t = r.a_full[:, :, cols].reshape(SEQ, 256)
            grads_t = r.d_full[:, :, cols].reshape(SEQ, 256)
            for g in range(2):
                grad_qkv = dot_tn(rows_t, r.dgu[g, :, :, 0:QKV].reshape(SEQ, QKV))
                r.w_attn[g, p // 2, p % 2, :, :, :, 0:QKV] = grad_qkv.reshape(2, 2, 64, QKV).astype(BF16)
                heads = r.os[g]
                mixed = jnp.concatenate(
                    [heads[:, :ROWS].reshape(SEQ, HEAD), heads[:, ROWS:].reshape(SEQ, HEAD)], axis=1
                )
                grad_o = dot_tn(grads_t, mixed)
                r.w_attn[g, p // 2, p % 2, :, :, :, QKV:AW] = grad_o.reshape(2, 2, 64, 256).astype(BF16)
        other = pl.ds(flip(core), 1)
        whole = (both, both, both, both)
        to_core = send(r.w_attn.at[(*whole, other)], r.core_in, "c")
        to_core.wait_recv()
        index = (*whole, lane)
        r.w_attn[index] = (r.w_attn[index].astype(F32) + r.core_in[...].astype(F32)).astype(BF16)
        tail["step"] = reduce_send(r.w_attn, "ra", 3, lane)

    mlp_back_x = rcopy(mlp_pair, r.mlp_x, "x")
    mlp_back_c = rcopy(r.mlp_sum.at[flip(core)], r.mlp_c, "c")
    da = square_sum(part_da, r.rs_q_n, r.rs_q_d, attn_grads)

    rows_x = rows_x_again(r)
    inv_a = row_scale(rows_x)
    scaled = da * attn_gain
    inner = jnp.mean(scaled * rows_x, axis=-1, keepdims=True)
    r.input_grad[...] = reorder(r.resid[...] + inv_a * scaled - rows_x * (inv_a * inv_a * inv_a * inner))

    step_a = tail["step"]
    reduce_add(r.w_attn, "ra", 3, lane, step_a)
    step_a = reduce_send(r.w_attn, "ra", 2, lane)

    @pl.when(carries)
    def _():
        mlp_back_x.wait_recv()
        r.mlp_sum[...] = mlp_pair[...].astype(F32) + r.mlp_x[...].astype(F32)
        mlp_back_c.start()

    links = ["c", "x", "y", "xo", "yo", "za", "zb"]

    def gain_send(n):
        return send(r.gains, r.gain_in.at[n], links[n])

    def gain_add(n, copy):
        copy.wait()
        unsent[:] = [other for other in unsent if other is not copy]
        r.gains[...] += r.gain_in[n]

    g_step = gain_send(0)
    reduce_add(r.w_attn, "ra", 2, lane, step_a)
    step_a = reduce_send(r.w_attn, "ra", 1, lane)
    gain_add(0, g_step)
    g_step = gain_send(1)
    gain_add(1, g_step)
    g_step = gain_send(2)
    reduce_add(r.w_attn, "ra", 1, lane, step_a)
    step_a = reduce_send(r.w_attn, "ra", 0, lane)
    gain_add(2, g_step)
    g_step = gain_send(3)

    @pl.when(lends)
    def _():
        mlp_back_c.wait_recv()
        r.d_mlp[...] = r.mlp_c[...]

    @pl.when(carries)
    def _():
        r.d_mlp[...] = r.mlp_sum[core]

    gain_add(3, g_step)
    g_step = gain_send(4)
    for part in range(4):
        rows = pl.ds(16 * part, 16)
        step_a[part].wait_recv()
        total = r.w_attn[(*own_slot(lane), rows)].astype(F32) + getattr(r, f"ra_{part}_0")[...].astype(F32)
        r.attn_sum[16 * part : 16 * part + 16] = total.reshape(16, AW)
    attn_back = rcopy(r.attn_sum, r.attn_x, "x")

    @pl.when(x_hi == 1)
    def _():
        attn_back.start()

    gain_add(4, g_step)
    g_step = gain_send(5)

    @pl.when(x_hi == 0)
    def _():
        r.d_attn[...] = r.attn_sum[...]

    gain_add(5, g_step)
    g_step = gain_send(6)

    @pl.when(x_hi == 1)
    def _():
        attn_back.wait_recv()
        r.d_attn[...] = r.attn_x[...]

    gain_add(6, g_step)
    sums = r.gains[...]
    inv_gain = 1.0 / attn_gain
    r.d_gain[...] = reorder(sums)
    r.d_gain[0:1] = reorder(sums[0:1] * inv_gain)
    r.d_gain[2:3] = sums[2:3]
    flush()

    @pl.when(x_hi == 1)
    def _():
        swap.wait_send()
        attn_back.wait_send()

    @pl.when(lends)
    def _():
        mlp_to_core.wait_send()
        mlp_back_x.wait_send()

    @pl.when(carries)
    def _():
        mlp_back_c.wait_send()


def rows_x_again(r):
    return reorder(r.tok[...].astype(F32))


def rope_tables():
    position = np.arange(SEQ, dtype=np.float32)[:, None]
    channel = np.arange(HEAD // 2, dtype=np.float32)[None, :]
    rate = np.exp(channel * np.float32(-2.0 * math.log(ROPE_BASE) / HEAD)).astype(np.float32)
    angle = (position * rate).astype(np.float32).astype(np.float64)
    cos = np.cos(angle).astype(np.float32)
    sin = np.sin(angle).astype(np.float32)
    shape = (4, ROWS, HEAD)
    return (
        np.concatenate([cos, cos], axis=1).reshape(shape),
        np.concatenate([-sin, sin], axis=1).reshape(shape),
    )


def body(
    tokens,
    attn_gain,
    w_query,
    key_weight,
    value_weight,
    query_gain,
    key_gain,
    w_out,
    mlp_gain,
    w_gate,
    w_up,
    w_down,
    out_cotangent,
):
    pack_attn = jnp.concatenate([w_query, key_weight, value_weight, w_out.T], axis=1)
    pack_mlp = jnp.concatenate([w_gate, w_up, w_down.T], axis=1)
    cosf, sinf = rope_tables()
    vmem = pl.BlockSpec(memory_space=pltpu.VMEM)
    layer_out, input_grad, d_attn, d_mlp, d_gain = pl.pallas_call(
        kernel,
        out_shape=(
            jax.ShapeDtypeStruct((ROWS, WIDTH), BF16),
            jax.ShapeDtypeStruct((ROWS, WIDTH), F32),
            jax.ShapeDtypeStruct((64, AW), F32),
            jax.ShapeDtypeStruct((64, MW), F32),
            jax.ShapeDtypeStruct((8, WIDTH), F32),
        ),
        in_specs=[vmem] * len(INPUTS),
        out_specs=(vmem,) * len(OUTPUTS),
        scratch_shapes=[pltpu.VMEM(*SCRATCH[name]) for name in NAMES]
        + [pltpu.SemaphoreType.DMA((N_SEM,)), pltpu.SemaphoreType.DMA((N_SEM,))],
        compiler_params=pltpu.CompilerParams(
            collective_id=0, has_side_effects=True, vmem_limit_bytes=64 * 2**20 - 2**17
        ),
        name="layer",
    )(
        tokens,
        out_cotangent,
        pack_attn,
        pack_mlp,
        attn_gain.reshape(1, -1),
        mlp_gain.reshape(1, -1),
        query_gain.reshape(1, -1),
        key_gain.reshape(1, -1),
        jnp.asarray(cosf),
        jnp.asarray(sinf),
    )
    return (
        layer_out,
        input_grad,
        d_gain[0],
        d_attn[:, 0:256],
        d_attn[:, 256:384],
        d_attn[:, 384:512],
        d_gain[2, 0:HEAD],
        d_gain[2, HEAD : 2 * HEAD],
        d_attn[:, 512:768].T,
        d_gain[1],
        d_mlp[:, 0:HID],
        d_mlp[:, HID : 2 * HID],
        d_mlp[:, 2 * HID : MW].T,
    )


def solution(mesh):
    rows = P(("dp", "tensor"), None)
    first = P("dp", "tensor")
    second = P("tensor", "dp")
    whole = P()
    return jax.shard_map(
        body,
        mesh=mesh,
        in_specs=(
            rows,
            whole,
            first,
            first,
            first,
            whole,
            whole,
            second,
            whole,
            first,
            first,
            second,
            rows,
        ),
        out_specs=(
            rows,
            rows,
            whole,
            first,
            first,
            first,
            whole,
            whole,
            second,
            whole,
            first,
            first,
            second,
        ),
        check_vma=False,
    )
```

time: 1360 us -> 220 us (0.16)
  waiting for transfers between devices: 809 us -> 0 us
  blocking collectives: 274 us -> 0 us
  Pallas kernels: 0 us -> 202 us
  matrix products: 138 us -> 0 us
  other arithmetic: 57.1 us -> 2.14 us
  local copies, waits for them, and re-layouts: 54.8 us -> 12.8 us
  between operations: 15 us -> 0.69 us
    reduce_scatter x11 -> x0, waiting for transfers between devices: 646 us -> none  [the longest x4 295 us: rows_sum(): lax.psum_scatter(partial_rows.astype(jnp.bfloat16), 'tensor', scatter_dim...]
    all_gather x7 -> x0, blocking collectives: 206 us -> none  [the longest x2 62.7 us: fetch_output(): return lax.all_gather(w_part, 'dp', axis=1, tiled=True)]
    pallas_call x0 -> x1, Pallas kernels: none -> 202 us  [body(): pl.pallas_call(kernel, out_shape=(jax.ShapeDtypeStruct((ROWS, WIDTH), BF1...]
    all_gather x4 -> x0, waiting for transfers between devices: 162 us -> none  [rows_gather(): return lax.all_gather(rows_part, 'tensor', axis=0, tiled=True)]
    dot_general x49 -> x0, matrix products: 138 us -> none  [the longest x7 38.7 us: dot_right_t(): lax.dot_general(first_op, second_op, (((1,), (1,)), ((), ())), preferred_...]
    psum x1 -> x0, blocking collectives: 67.3 us -> none  [body(): lax.psum((jnp.sum(attn_gain_part, axis=0), jnp.sum(mlp_gain_part, axis=0)...]
    convert_element_type x15 -> x0, other arithmetic: 19.5 us -> none  [the longest x3 4.06 us: body(): w_query_grad, w_key_grad, w_value_grad = (lax.psum_scatter(dot_left_t(att...]
    reduce_sum x12 -> x0, other arithmetic: 14.4 us -> none  [the longest x3 5.76 us: rms_scale(): jnp.mean(values * values, axis=-1, keepdims=True) + eps_norm]
  transfers between devices with their start and end apart: 15 -> 0, of which waited for: 13 -> 0; matrix products, arithmetic and copies ran while one was open for 12% -> 0% of each run, Pallas kernels for 0% -> 0%
where the time goes in v1:
time: 220 us; the launch traced here: 218 us
  Pallas kernels  202 us (92%)
  local copies, waits for them, and re-layouts  12.8 us (6%)
    pallas_call x1, Pallas kernels, body(): pl.pallas_call(kernel, out_shape=(jax.ShapeDtypeStruct((ROWS, WIDTH), BF1...  202 us

profile of v1, /device:TPU:8, one launch (start us, length us, event | category | flops | bytes accessed | tf_op | source)
XLA Modules:
  0.0 217.7 jit_solution(14855735483765024331)
XLA Ops:
  0.6 0.0 copy-start.4
  0.7 1.3 reshape.38.refs_4_
  1.9 1.3 reshape.39.refs_5_
  3.2 0.0 copy-done.4
  3.2 0.0 copy-start.1
  3.2 0.0 copy-start.2
  3.2 0.0 copy-start.3
  3.2 1.5 pad_maximum_fusion.1.refs_2_
  4.7 0.0 copy-done.1
  4.7 0.0 copy-done.2
  4.7 0.0 copy-done.3
  4.7 0.7 pad_maximum_fusion.refs_3_
  5.4 202.1 %layer.1 = (bf16[256,1024]{1,0:T(8,128)(2,1)}, f32[256,1024]{1,0:T(8,128)}, f32[64,768]{1,0:T(8,128)}, f32[64,1152]{1,0:T(8,128)}, f32[8,1024]{1,0:T(8,128)}) custom-call(bf16[256,1024]{1,0:T(8,128)(2,1)} %refs_0_.1, bf16[256,1024]{1,0:T(8,128)(2,1)} %refs_1_.1, bf16[64,768]{1,0:T(8,128)(2,1)} %pad_maximum_fusion.1.refs_2_, ...), custom_call_target="tpu_custom_call" | custom-call | tf_op jit(solution)/shard_map/layer/pallas_call | solution.py:789
  207.5 0.0 copy-start
  207.5 1.3 slice_bitcast_fusion.2
  208.8 1.4 fusion.1
  210.2 1.4 fusion
  211.6 1.5 slice_bitcast_fusion.1
  213.2 1.7 slice_bitcast_fusion
  214.9 1.9 copy.30
  216.7 0.0 copy-done
  216.7 1.0 copy.31
Async XLA Ops:
  0.6 2.6 %copy-start.4 = (bf16[64,128]{1,0:T(8,128)(2,1)S(1)}, bf16[64,128]{1,0:T(8,128)(2,1)}, u32[]{:S(2)}) copy-start(bf16[64,128]{1,0:T(8,128)(2,1)} %param.19) | copy-start | bytes 49156
  3.2 1.5 copy-start.1
  3.2 1.5 copy-start.2
  3.2 1.5 copy-start.3
  207.5 9.2 %copy-start = (f32[256,1024]{1,0:T(8,128)S(1)}, f32[256,1024]{1,0:T(8,128)}, u32[]{:S(2)}) copy-start(f32[256,1024]{1,0:T(8,128)} %get-tuple-element.48) | copy-start | bytes 3145732

commit v2 on v1

v2 whole, which is shorter than its diff:
```python
import math

import jax
import jax.numpy as jnp
import numpy as np
from jax import lax
from jax.experimental import pallas as pl
from jax.experimental.pallas import tpu as pltpu
from jax.sharding import PartitionSpec as P

HEAD = 128
SEQ = 1024
WIDTH = 1024
ROWS = 256
QKV = 512
OW = 256
AW = QKV + OW
HID = 384
MW = 3 * HID
EPS = 1e-06
ROPE_BASE = 1000000.0
EXP_SCALE = math.log2(math.e) / math.sqrt(HEAD)
SCORE_SCALE = 1.0 / math.sqrt(HEAD)
MESH = pl.DeviceIdType.MESH
F32 = jnp.float32
BF16 = jnp.bfloat16


def dot_nn(a, b):
    return jnp.dot(a, b, preferred_element_type=F32)


def dot_nt(a, b):
    return lax.dot_general(a, b, (((1,), (1,)), ((), ())), preferred_element_type=F32)


def dot_tn(a, b):
    return lax.dot_general(a, b, (((0,), (0,)), ((), ())), preferred_element_type=F32)


def reorder(v):
    return jnp.concatenate([v[:, :512], v[:, 768:], v[:, 512:768]], axis=1)


def row_scale(v):
    return lax.rsqrt(jnp.mean(v * v, axis=-1, keepdims=True) + EPS)


def flip(bit):
    return 1 - bit


SCRATCH = {
    "w_q": ((2, 2, 2, 2, 2, 64, QKV), BF16),
    "w_o": ((2, 2, 2, 2, 2, 64, OW), BF16),
    "w_m": ((2, 2, 2, 2, 2, 64, MW), BF16),
    "pack_q": ((64, QKV), BF16),
    "pack_o": ((64, OW), BF16),
    "pack_m": ((64, MW), BF16),
    "a_full": ((4, ROWS, WIDTH), BF16),
    "m_full": ((4, ROWS, WIDTH), BF16),
    "c_full": ((4, ROWS, WIDTH), BF16),
    "d_full": ((4, ROWS, WIDTH), BF16),
    "qkp": ((2, 4, ROWS, 384), F32),
    "qs": ((2, 4, 512, HEAD), BF16),
    "ks": ((2, 4, ROWS, HEAD), BF16),
    "kt": ((2, 4, HEAD, ROWS), BF16),
    "vs": ((2, 4, ROWS, HEAD), BF16),
    "vt": ((2, 4, HEAD, ROWS), BF16),
    "os": ((2, 4, 512, HEAD), BF16),
    "linv": ((2, 4, 8, 512), F32),
    "dos": ((2, 512, HEAD), BF16),
    "dk": ((2, 4, ROWS, HEAD), F32),
    "dv": ((2, 4, ROWS, HEAD), F32),
    "hid": ((2, 4, ROWS, HID), BF16),
    "dgu": ((2, 4, ROWS, 2 * HID), BF16),
    "own": ((ROWS, WIDTH), F32),
    "own_down": ((ROWS, WIDTH), F32),
    "resid": ((ROWS, WIDTH), F32),
    "stage": ((3, ROWS, WIDTH), BF16),
    "stage_down": ((3, ROWS, WIDTH), BF16),
    "far": ((2, 128, WIDTH), BF16),
    "near": ((2, ROWS, WIDTH), BF16),
    "sum_m": ((3, ROWS, WIDTH), BF16),
    "sum_d": ((3, ROWS, WIDTH), BF16),
    "gains": ((8, WIDTH), F32),
    "gain_in": ((7, 8, WIDTH), F32),
    "core_q": ((2, 2, 2, 2, 1, 64, QKV), BF16),
    "core_o": ((2, 2, 2, 2, 1, 64, OW), BF16),
    "mlp_x": ((2, 64, MW), BF16),
    "mlp_c": ((64, MW), F32),
    "attn_x": ((64, AW), F32),
    "attn_sum": ((64, AW), F32),
    "mlp_sum": ((2, 64, MW), F32),
}
AXES = {"xo": 3, "yo": 0, "za": 2, "zb": 1}
ORDER = ["xo", "yo", "za", "zb"]


def part_axes(part):
    return [ORDER[(part + step) % 4] for step in range(4)]


def cube_shape(part, step, cores, width):
    shape = [1, 1, 1, 1]
    for axis in part_axes(part)[:step]:
        shape[AXES[axis]] = 2
    return (*shape, cores, 16, width)


for _part in range(4):
    for _step in range(4):
        SCRATCH[f"sum_q_{_part}_{_step}"] = (cube_shape(_part, _step, 1, QKV), BF16)
        SCRATCH[f"sum_o_{_part}_{_step}"] = (cube_shape(_part, _step, 1, OW), BF16)
        SCRATCH[f"sum_w_{_part}_{_step}"] = (cube_shape(_part, _step, 2, MW), BF16)

NAMES = list(SCRATCH)
N_SEM = 107
INPUTS = ["tok", "cot", "wq", "wk", "wv", "wo", "wg", "wu", "wd", "ag", "mg", "qg", "kg", "cosf", "sinf"]
OUTPUTS = ["layer_out", "input_grad", "d_attn", "d_mlp", "d_gain"]


class Refs:
    pass


class Copy:
    def __init__(self, copy, gives, takes):
        self.copy, self.gives, self.takes = copy, gives, takes
        self.started = self.received = self.sent = False

    def run(self, cond, act):
        if cond is None:
            act()
        else:
            pl.when(cond)(act)

    def start(self):
        self.started = True
        self.run(self.gives, self.copy.start)

    def wait_recv(self):
        self.received = True
        self.run(self.takes, self.copy.wait_recv)

    def wait_send(self):
        self.sent = True
        self.run(self.gives, self.copy.wait_send)


def kernel(*refs):
    r = Refs()
    names = INPUTS + OUTPUTS + NAMES
    for name, ref in zip(names, refs):
        setattr(r, name, ref)
    ssem, rsem = refs[len(names)], refs[len(names) + 1]

    dp = lax.axis_index("dp")
    tn = lax.axis_index("tensor")
    z = dp // 4
    x_hi = (dp // 2) % 2
    core = dp % 2
    y = tn // 2
    x_lo = tn % 2
    y_lo = y % 2
    y_hi = y // 2
    gz = jnp.where(z < 2, z, 5 - z)
    own_bit = {"xo": x_hi, "yo": y_hi, "za": gz % 2, "zb": gz // 2}
    nbr = {
        "c": (dp + 1 - 2 * core, tn),
        "x": (dp, tn + 1 - 2 * x_lo),
        "y": (dp, tn + 2 - 4 * y_lo),
        "xo": (dp + 2 - 4 * x_hi, tn + 1 - 2 * x_lo),
        "yo": (dp, (3 - y) * 2 + x_lo),
        "za": (dp + 4 - 8 * (z % 2), tn),
        "zb": (dp + 4 * (3 - 2 * z), tn),
    }
    pair = "y"

    def square(k):
        kx, ky = k % 2, k // 2
        return (y_lo + ky - 2 * y_lo * ky) * 2 + x_lo + kx - 2 * x_lo * kx

    def group(k):
        kc = k % 2
        return (k // 2) * 2 + core + kc - 2 * core * kc

    ids = {}
    copies = r.copies = []
    unsent = []

    def later(src, dst, to, key, gives=None, takes=None):
        i = ids.setdefault(key, len(ids))
        copy = pltpu.make_async_remote_copy(
            src_ref=src,
            dst_ref=dst,
            send_sem=ssem.at[i],
            recv_sem=rsem.at[i],
            device_id=nbr[to],
            device_id_type=MESH,
        )
        copies.append(Copy(copy, gives, takes))
        unsent.append(copies[-1])
        return copies[-1]

    def send(*args, **kinds):
        copy = later(*args, **kinds)
        copy.start()
        return copy

    def flush():
        for copy in unsent:
            if copy.started and not copy.sent:
                copy.wait_send()
        unsent[:] = [copy for copy in unsent if not copy.sent]

    def wait_recv(group):
        for copy in group:
            copy.wait_recv()

    def at(k, value, act):
        pl.when(k == value)(act)

    def slots(full, current, cores):
        index = [None] * 4
        for axis in ORDER:
            if axis in full:
                index[AXES[axis]] = pl.ds(0, 2)
            else:
                bit = own_bit[axis]
                index[AXES[axis]] = pl.ds(flip(bit) if current == axis else bit, 1)
        return (*index, cores)

    both = pl.ds(0, 2)
    lane = pl.ds(core, 1)
    lanes = {"q": lane, "o": lane, "w": both}
    weights = {"q": r.w_q, "o": r.w_o, "w": r.w_m}
    own_slot = (own_bit["yo"], own_bit["zb"], own_bit["za"], own_bit["xo"])
    own_view = tuple(pl.ds(bit, 1) for bit in own_slot)

    def step_key(kind, part, step, back):
        return (kind, part, step, back and kind == "w" and step == 3)

    def gather_step(kind, step):
        out = []
        for part in range(4):
            axes = part_axes(part)
            rows = pl.ds(16 * part, 16)
            view = weights[kind].at[(*slots(axes[:step], None, lanes[kind]), rows)]
            out.append(send(view, view, axes[step], step_key(kind, part, step, False)))
        return out

    def core_send(kind, late):
        out = []
        for part in range(4):
            axes = part_axes(part)
            rows = pl.ds(16 * part, 16)
            view = weights[kind].at[(*slots(axes[:3], axes[3] if late else None, lane), rows)]
            out.append(send(view, view, "c", ("core", kind, late, part)))
        return out

    def reduce_later(kind, step):
        out = []
        for part in range(4):
            axes = part_axes(part)
            rows = pl.ds(16 * part, 16)
            view = weights[kind].at[(*slots(axes[:step], axes[step], lanes[kind]), rows)]
            buf = getattr(r, f"sum_{kind}_{part}_{step}")
            out.append(later(view, buf, axes[step], step_key(kind, part, step, True)))
        return out

    def start(group):
        for copy in group:
            copy.start()

    def reduce_add(kind, step, group):
        for part in range(4):
            axes = part_axes(part)
            rows = pl.ds(16 * part, 16)
            index = (*slots(axes[:step], None, lanes[kind]), rows)
            group[part].wait_recv()
            total = weights[kind][index].astype(F32) + getattr(r, f"sum_{kind}_{part}_{step}")[...].astype(F32)
            weights[kind][index] = total.astype(BF16)

    barrier = pltpu.get_barrier_semaphore()
    for to in nbr:
        pl.semaphore_signal(barrier, inc=1, device_id=nbr[to], device_id_type=MESH)

    carries = core == x_lo
    lends = core != x_lo
    r.pack_q[:, 0:256] = r.wq[...]
    r.pack_q[:, 256:384] = r.wk[...]
    r.pack_q[:, 384:512] = r.wv[...]
    r.pack_o[...] = r.wo[...]
    r.pack_m[:, 0:HID] = r.wg[...]
    r.pack_m[:, HID : 2 * HID] = r.wu[...]
    r.pack_m[:, 2 * HID : MW] = r.wd[...]

    @pl.when(x_hi == 0)
    def _():
        r.w_q[(*own_view, lane)] = r.pack_q[...].reshape(1, 1, 1, 1, 1, 64, QKV)
        r.w_o[(*own_view, lane)] = r.pack_o[...].reshape(1, 1, 1, 1, 1, 64, OW)

    @pl.when(carries)
    def _():
        r.w_m[(*own_view, lane)] = r.pack_m[...].reshape(1, 1, 1, 1, 1, 64, MW)

    attn_gain = reorder(r.ag[...].astype(F32).reshape(1, WIDTH))
    mlp_gain = reorder(r.mg[...].astype(F32).reshape(1, WIDTH))
    query_gain = r.qg[...].astype(F32).reshape(1, HEAD)
    key_gain = r.kg[...].astype(F32).reshape(1, HEAD)

    def rows_in():
        return reorder(r.tok[...].astype(F32))

    rows_x = rows_in()
    r.a_full[square(0)] = (rows_x * row_scale(rows_x) * attn_gain).astype(BF16)
    r.c_full[group(0)] = reorder(r.cot[...])
    pl.semaphore_wait(barrier, len(nbr))

    swap_q = send(r.pack_q, r.w_q.at[(*own_slot, core)], "x", "swap_q", gives=x_hi == 1, takes=x_hi == 1)
    swap_o = send(r.pack_o, r.w_o.at[(*own_slot, core)], "x", "swap_o", gives=x_hi == 1, takes=x_hi == 1)
    mlp_pair = r.w_m.at[own_slot]
    mlp_to_core = send(r.pack_m, r.w_m.at[(*own_slot, core)], "c", "mlp_c", gives=lends, takes=carries)
    mlp_to_x = later(mlp_pair, mlp_pair, "x", "mlp_x", gives=carries, takes=lends)

    def square_gather(buf):
        def half(k, n):
            return buf.at[square(k), pl.ds(128 * n, 128)]

        x0 = send(half(0, 0), half(0, 0), "x", "sg_x0")
        y1 = send(half(0, 1), half(0, 1), "y", "sg_y1")
        x1 = send(half(0, 1), half(0, 1), "x", "sg_x1")
        y0 = send(half(0, 0), half(0, 0), "y", "sg_y0")
        fy = later(half(1, 0), half(1, 0), "y", "sg_fy")
        fx = later(half(2, 1), half(2, 1), "x", "sg_fx")

        def forward():
            x0.wait_recv()
            fy.start()
            y1.wait_recv()
            fx.start()

        return forward, x1, y0, [fx, fy]

    a_forward, a_x1, a_y0, a_far = square_gather(r.a_full)

    swap_q.wait_recv()
    step_q = gather_step("q", 0)
    wait_recv(step_q)
    step_q = gather_step("q", 1)
    swap_o.wait_recv()
    step_o = gather_step("o", 0)
    mlp_to_core.wait_recv()
    mlp_to_x.start()
    a_forward()
    wait_recv(step_q)
    step_q = gather_step("q", 2)
    wait_recv(step_o)
    step_o = gather_step("o", 1)
    wait_recv(step_q)
    step_q = gather_step("q", 3)
    early = core_send("q", False)
    wait_recv(step_o)
    step_o = gather_step("o", 2)
    mlp_to_x.wait_recv()
    step_w = gather_step("w", 0)
    wait_recv(step_q)
    late = core_send("q", True)
    wait_recv(step_o)
    step_o = gather_step("o", 3)
    early_o = core_send("o", False)
    wait_recv(early)
    wait_recv(late)

    def w_qkv(g):
        return r.w_q[g].reshape(WIDTH, QKV)

    def w_out(g):
        return r.w_o[g].reshape(WIDTH, OW)

    def w_gu(g):
        return r.w_m[g, :, :, :, :, :, 0 : 2 * HID].reshape(WIDTH, 2 * HID)

    def w_dn(g):
        return r.w_m[g, :, :, :, :, :, 2 * HID : MW].reshape(WIDTH, HID)

    c_pair = later(r.c_full.at[group(0)], r.c_full.at[core + 2], pair, "cot_p")
    c_core = later(r.c_full.at[group(0)], r.c_full.at[group(0)], "c", "cot_c")

    def qkv_block(k, carry):
        at(k, 1, a_x1.wait_recv)
        at(k, 2, a_y0.wait_recv)

        @pl.when(k == 3)
        def _():
            wait_recv(a_far)
            c_pair.start()
            c_core.start()

        blk = square(k)
        rows = r.a_full[blk]
        cos = r.cosf[blk]
        sin = r.sinf[blk]
        for g in range(2):
            acc = dot_nn(rows, w_qkv(g))
            r.qkp[g, blk] = acc[:, :384]
            for h in range(3):
                pre = acc[:, h * HEAD : (h + 1) * HEAD]
                normed = pre * row_scale(pre) * (key_gain if h == 2 else query_gain)
                turned = normed * cos + pltpu.roll(normed, 64, 1) * sin
                if h == 2:
                    r.ks[g, blk] = turned.astype(BF16)
                    r.kt[g, blk] = turned.T.astype(BF16)
                else:
                    r.qs[g, blk, h * ROWS : (h + 1) * ROWS] = turned.astype(BF16)
            value = acc[:, 384:]
            r.vs[g, blk] = value.astype(BF16)
            r.vt[g, blk] = value.T.astype(BF16)
        return carry

    lax.fori_loop(0, 4, qkv_block, 0)
    wait_recv(step_w)
    step_w = gather_step("w", 1)
    wait_recv(step_o)
    late_o = core_send("o", True)

    key_at = lax.broadcasted_iota(jnp.int32, (ROWS, 512), 0)
    query_at = lax.broadcasted_iota(jnp.int32, (ROWS, 512), 1) % ROWS
    visible = key_at <= query_at

    def weights_t(g, i, j, diagonal):
        scores = dot_nt(r.ks[g, j], r.qs[g, i])
        exps = jnp.exp2(scores * EXP_SCALE)
        if diagonal:
            exps = jnp.where(visible, exps, 0.0)
        return exps

    def attend_step(i, j, carry, diagonal):
        out = []
        for g in range(2):
            total, acc = carry[g]
            exps = weights_t(g, i, j, diagonal)
            total = total + jnp.sum(exps, axis=0, keepdims=True)
            acc = acc + dot_nn(r.vt[g, j], exps.astype(BF16))
            out.append((total, acc))
        return tuple(out)

    def attend_block(i):
        zero = (jnp.zeros((1, 512), F32), jnp.zeros((HEAD, 512), F32))
        state = lax.fori_loop(0, i, lambda j, s: attend_step(i, j, s, False), (zero, zero))
        state = attend_step(i, i, state, True)
        for g in range(2):
            total, acc = state[g]
            inv = 1.0 / total
            r.linv[g, i] = jnp.broadcast_to(inv, (8, 512))
            r.os[g, i] = (acc * inv).T.astype(BF16)

    def part_o(blk):
        acc = jnp.zeros((ROWS, WIDTH), F32)
        for g in range(2):
            heads = r.os[g, blk]
            acc = acc + dot_nt(jnp.concatenate([heads[:ROWS], heads[ROWS:]], axis=1), w_out(g))
        return acc

    def square_sum(part_of, steps):
        def out(n, rows, buf, to, key):
            return later(r.stage.at[n, pl.ds(*rows)], buf, to, key)

        low, high = (0, 128), (128, 128)
        d0 = out(2, low, r.far.at[0], "x", "ss_d0")
        d1 = out(2, high, r.far.at[1], "y", "ss_d1")
        x0 = out(0, low, r.near.at[0, pl.ds(*low)], "x", "ss_x0")
        x1 = out(0, high, r.near.at[0, pl.ds(*high)], "x", "ss_x1")
        y0 = out(1, low, r.near.at[1, pl.ds(*low)], "y", "ss_y0")
        y1 = out(1, high, r.near.at[1, pl.ds(*high)], "y", "ss_y1")

        def block(n, carry):
            k = jnp.where(n == 0, 3, n % 3)
            for value, act in steps.items():
                at(n, value, act)
            acc = part_of(square(k))

            @pl.when(n < 3)
            def _():
                r.stage[(n + 2) % 3] = acc.astype(BF16)

            @pl.when(n == 3)
            def _():
                r.own[...] = acc

            @pl.when(n == 0)
            def _():
                d0.start()
                d1.start()

            at(n, 1, x0.start)
            at(n, 2, y1.start)
            return carry

        lax.fori_loop(0, 4, block, 0)
        d1.wait_recv()
        r.stage[0, 128:256] = (r.stage[0, 128:256].astype(F32) + r.far[1].astype(F32)).astype(BF16)
        x1.start()
        d0.wait_recv()
        r.stage[1, 0:128] = (r.stage[1, 0:128].astype(F32) + r.far[0].astype(F32)).astype(BF16)
        y0.start()

        def finish():
            wait_recv([x0, y1, x1, y0])
            return r.own[...] + r.near[0].astype(F32) + r.near[1].astype(F32)

        return finish

    def attend_and_part(blk):
        attend_block(blk)
        return part_o(blk)

    wait_recv(early_o)
    wait_recv(late_o)
    wait_recv(step_w)
    step_w = gather_step("w", 2)
    o_finish = square_sum(attend_and_part, {})
    wait_recv(step_w)
    step_w = gather_step("w", 3)
    c_pair.wait_recv()
    c_forward = send(r.c_full.at[core + 2], r.c_full.at[core + 2], "c", "cot_f")
    resid = rows_in() + o_finish()
    r.resid[...] = resid

    r.m_full[group(0)] = (resid * row_scale(resid) * mlp_gain).astype(BF16)
    m_pair = []
    m_forward = []
    for n in range(2):
        rows = pl.ds(128 * n, 128)
        m_pair.append(send(r.m_full.at[group(0), rows], r.m_full.at[core + 2, rows], pair, ("m_p", n)))
        m_forward.append(later(r.m_full.at[core + 2, rows], r.m_full.at[core + 2, rows], "c", ("m_f", n)))
    m_core = send(r.m_full.at[group(0)], r.m_full.at[group(0)], "c", "m_c")
    wait_recv(step_w)
    wait_recv([c_core, c_forward])

    def mlp_block(k, carry):
        at(k, 1, m_core.wait_recv)

        @pl.when(k == 2)
        def _():
            for n in range(2):
                m_pair[n].wait_recv()
                m_forward[n].start()

        @pl.when(k == 3)
        def _():
            wait_recv(m_forward)

        i = group(k)
        rows = r.m_full[i]
        cots = r.c_full[i]
        for g in range(2):
            pre = dot_nn(rows, w_gu(g))
            grad = dot_nn(cots, w_dn(g))
            gate = pre[:, :HID]
            up = pre[:, HID:]
            sig = 1.0 / (1.0 + jnp.exp(-gate))
            act = gate * sig
            r.hid[g, i] = (act * up).astype(BF16)
            r.dgu[g, i, :, 0:HID] = (grad * up * sig * (1.0 + gate * (1.0 - sig))).astype(BF16)
            r.dgu[g, i, :, HID : 2 * HID] = (grad * act).astype(BF16)
        return carry

    lax.fori_loop(0, 4, mlp_block, 0)
    flush()

    def pair_sum(part_of, stage, recv, own, name, hold):
        s3 = later(stage.at[2], recv.at[0], "c", (name, 3))
        s1 = later(stage.at[0], recv.at[1], "c", (name, 1))
        s2 = later(stage.at[1], recv.at[2], pair, (name, 2))

        def block(n, carry):
            acc = part_of(group(3 - n))

            @pl.when(n == 0)
            def _():
                stage[2] = acc.astype(BF16)
                s3.start()

            @pl.when(n == 1)
            def _():
                s3.wait_recv()
                stage[1] = (acc + recv[0].astype(F32)).astype(BF16)
                if not hold:
                    s2.start()

            @pl.when(n == 2)
            def _():
                stage[0] = acc.astype(BF16)
                s1.start()

            @pl.when(n == 3)
            def _():
                own[...] = acc

            return carry

        lax.fori_loop(0, 4, block, 0)

        def finish():
            wait_recv([s1, s2])
            return own[...] + recv[1].astype(F32) + recv[2].astype(F32)

        return finish, s2

    def part_dm(i):
        return dot_nt(r.dgu[0, i], w_gu(0)) + dot_nt(r.dgu[1, i], w_gu(1))

    def part_down(i):
        return dot_nt(r.hid[0, i], w_dn(0)) + dot_nt(r.hid[1, i], w_dn(1))

    dm_finish, _ = pair_sum(part_dm, r.stage, r.sum_m, r.own, "dm", False)
    down_finish, down_pair = pair_sum(part_down, r.stage_down, r.sum_d, r.own_down, "down", True)
    r.own_down[...] += r.resid[...]

    def mlp_grads(p, carry):
        cols = pl.ds(pl.multiple_of(256 * p, 256), 256)
        rows_t = r.m_full[:, :, cols].reshape(SEQ, 256)
        cots_t = r.c_full[:, :, cols].reshape(SEQ, 256)
        for g in range(2):
            grad_gu = dot_tn(rows_t, r.dgu[g].reshape(SEQ, 2 * HID))
            grad_dn = dot_tn(cots_t, r.hid[g].reshape(SEQ, HID))
            r.w_m[g, p // 2, p % 2, :, :, :, 0 : 2 * HID] = grad_gu.reshape(2, 2, 64, 2 * HID).astype(BF16)
            r.w_m[g, p // 2, p % 2, :, :, :, 2 * HID : MW] = grad_dn.reshape(2, 2, 64, HID).astype(BF16)
        return carry

    lax.fori_loop(0, 4, mlp_grads, 0)
    back_w = {step: reduce_later("w", step) for step in range(4)}
    start(back_w[3])

    dm = dm_finish()
    resid = r.resid[...]
    inv_m = row_scale(resid)
    scaled = dm * mlp_gain
    inner = jnp.mean(scaled * resid, axis=-1, keepdims=True)
    r.gains[...] = jnp.zeros((8, WIDTH), F32)
    r.gains[1:2] = jnp.sum(dm * resid * inv_m, axis=0, keepdims=True)
    dresid = reorder(r.cot[...].astype(F32)) + inv_m * scaled - resid * (inv_m * inv_m * inv_m * inner)
    r.resid[...] = dresid
    r.d_full[square(0)] = dresid.astype(BF16)
    d_forward, d_x1, d_y0, d_far = square_gather(r.d_full)
    r.dk[...] = jnp.zeros((2, 4, ROWS, HEAD), F32)
    r.dv[...] = jnp.zeros((2, 4, ROWS, HEAD), F32)

    def back_step(i, j, carry, diagonal, delta):
        out = []
        for g in range(2):
            probs = weights_t(g, i, j, diagonal) * r.linv[g, i, 0:1]
            grads = dot_nt(r.vs[g, j], r.dos[g])
            dz = (probs * (grads - delta[g])).astype(BF16)
            r.dv[g, j] += dot_nn(probs.astype(BF16), r.dos[g])
            r.dk[g, j] += dot_nn(dz, r.qs[g, i])
            out.append(carry[g] + dot_nn(r.kt[g, j], dz))
        return tuple(out)

    def unnorm(pre, gain, grad):
        inv = row_scale(pre)
        hat = pre * inv
        scaled = grad * gain
        back = inv * (scaled - hat * jnp.mean(scaled * hat, axis=-1, keepdims=True))
        return back.astype(BF16), jnp.sum(grad * hat, axis=0, keepdims=True)

    def turn_back(grad, blk):
        return grad * r.cosf[blk] - pltpu.roll(grad, 64, 1) * r.sinf[blk]

    def back_block(k, gain_sum):
        @pl.when(k == 1)
        def _():
            d_forward()
            down_pair.start()
            d_x1.wait_recv()
            reduce_add("w", 3, back_w[3])
            start(back_w[2])

        at(k, 2, d_y0.wait_recv)

        @pl.when(k == 3)
        def _():
            wait_recv(d_far)
            reduce_add("w", 2, back_w[2])
            start(back_w[1])

        i = square(k)
        rows = r.d_full[i]
        delta = []
        for g in range(2):
            grad = dot_nn(rows, w_out(g))
            inner = []
            for h in range(2):
                part = grad[:, h * HEAD : (h + 1) * HEAD].astype(BF16)
                r.dos[g, h * ROWS : (h + 1) * ROWS] = part
                prod = part.astype(F32) * r.os[g, i, h * ROWS : (h + 1) * ROWS].astype(F32)
                inner.append(jnp.sum(prod.T, axis=0, keepdims=True))
            delta.append(jnp.concatenate(inner, axis=1))
        zero = jnp.zeros((HEAD, 512), F32)
        state = lax.fori_loop(0, i, lambda j, s: back_step(i, j, s, False, delta), (zero, zero))
        state = back_step(i, i, state, True, delta)
        for g in range(2):
            for h in range(2):
                grad = turn_back(state[g][:, h * ROWS : (h + 1) * ROWS].T * SCORE_SCALE, i)
                low, part = unnorm(r.qkp[g, i, :, h * HEAD : (h + 1) * HEAD], query_gain, grad)
                r.dgu[g, i, :, h * HEAD : (h + 1) * HEAD] = low
                gain_sum = gain_sum + part
        return gain_sum

    q_gain_part = lax.fori_loop(0, 4, back_block, jnp.zeros((1, HEAD), F32))

    other = pl.ds(flip(core), 1)
    whole = (both, both, both, both)

    def out_grads(p, carry):
        cols = pl.ds(pl.multiple_of(256 * p, 256), 256)
        grads_t = r.d_full[:, :, cols].reshape(SEQ, 256)
        for g in range(2):
            heads = r.os[g]
            mixed = jnp.concatenate(
                [heads[:, :ROWS].reshape(SEQ, HEAD), heads[:, ROWS:].reshape(SEQ, HEAD)], axis=1
            )
            r.w_o[g, p // 2, p % 2] = dot_tn(grads_t, mixed).reshape(2, 2, 64, OW).astype(BF16)
        return carry

    def core_sum(kind, buf, copy):
        copy.wait_recv()
        index = (*whole, lane)
        total = weights[kind][index].astype(F32) + buf[...].astype(F32)
        weights[kind][index] = total.astype(BF16)

    lax.fori_loop(0, 4, out_grads, 0)
    o_core = send(r.w_o.at[(*whole, other)], r.core_o, "c", "o_core")

    def key_block(j, gain_sum):
        for g in range(2):
            grad = turn_back(r.dk[g, j] * SCORE_SCALE, j)
            low, part = unnorm(r.qkp[g, j, :, 256:384], key_gain, grad)
            r.dgu[g, j, :, 256:384] = low
            r.dgu[g, j, :, 384:512] = r.dv[g, j].astype(BF16)
            gain_sum = gain_sum + part
        return gain_sum

    k_gain_part = lax.fori_loop(0, 4, key_block, jnp.zeros((1, HEAD), F32))
    r.gains[2:3, 0:HEAD] = q_gain_part
    r.gains[2:3, HEAD : 2 * HEAD] = k_gain_part
    flush()

    def part_da(blk):
        acc = dot_nt(r.dgu[0, blk, :, 0:QKV], w_qkv(0)) + dot_nt(r.dgu[1, blk, :, 0:QKV], w_qkv(1))
        r.gains[0:1] += jnp.sum(acc * r.a_full[blk].astype(F32), axis=0, keepdims=True)
        return acc

    back_o = {step: reduce_later("o", step) for step in range(4)}
    back_q = {step: reduce_later("q", step) for step in range(4)}

    def tail_o():
        core_sum("o", r.core_o, o_core)
        start(back_o[3])

    def tail_w():
        reduce_add("w", 1, back_w[1])
        start(back_w[0])

    a_finish = square_sum(part_da, {1: tail_o, 2: tail_w})

    def qkv_grads(p, carry):
        cols = pl.ds(pl.multiple_of(256 * p, 256), 256)
        rows_t = r.a_full[:, :, cols].reshape(SEQ, 256)
        for g in range(2):
            grad = dot_tn(rows_t, r.dgu[g, :, :, 0:QKV].reshape(SEQ, QKV))
            r.w_q[g, p // 2, p % 2] = grad.reshape(2, 2, 64, QKV).astype(BF16)
        return carry

    links = ["c", "za", "zb", "yo", "xo", "y", "x"]

    def gain_send(n):
        return send(r.gains, r.gain_in.at[n], links[n], ("gain", n))

    def gain_add(n, copy):
        copy.wait_send()
        copy.wait_recv()
        r.gains[...] += r.gain_in[n]

    g_step = gain_send(0)
    lax.fori_loop(0, 4, qkv_grads, 0)
    q_core = send(r.w_q.at[(*whole, other)], r.core_q, "c", "q_core")
    gain_add(0, g_step)
    g_step = gain_send(1)
    reduce_add("o", 3, back_o[3])
    start(back_o[2])
    core_sum("q", r.core_q, q_core)
    start(back_q[3])
    gain_add(1, g_step)
    g_step = gain_send(2)
    mlp_back_x = later(mlp_pair, r.mlp_x, "x", "mlp_x", gives=lends, takes=carries)
    mlp_back_c = later(r.mlp_sum.at[flip(core)], r.mlp_c, "c", "mlp_c", gives=carries, takes=lends)
    reduce_add("w", 0, back_w[0])
    mlp_back_x.start()
    reduce_add("o", 2, back_o[2])
    start(back_o[1])
    r.layer_out[...] = reorder(down_finish()).astype(BF16)
    gain_add(2, g_step)
    g_step = gain_send(3)
    reduce_add("q", 3, back_q[3])
    start(back_q[2])
    reduce_add("o", 1, back_o[1])
    start(back_o[0])
    gain_add(3, g_step)
    g_step = gain_send(4)
    reduce_add("q", 2, back_q[2])
    start(back_q[1])
    mlp_back_x.wait_recv()

    @pl.when(carries)
    def _():
        r.mlp_sum[...] = mlp_pair[...].astype(F32) + r.mlp_x[...].astype(F32)

    mlp_back_c.start()
    gain_add(4, g_step)

    rows_x = rows_in()
    inv_a = row_scale(rows_x)
    scaled = a_finish() * attn_gain
    g_step = gain_send(5)
    inner = jnp.mean(scaled * rows_x, axis=-1, keepdims=True)
    r.input_grad[...] = reorder(r.resid[...] + inv_a * scaled - rows_x * (inv_a * inv_a * inv_a * inner))
    reduce_add("q", 1, back_q[1])
    start(back_q[0])
    gain_add(5, g_step)
    g_step = gain_send(6)

    def last_step(kind, group, cols):
        for part in range(4):
            rows = pl.ds(16 * part, 16)
            group[part].wait_recv()
            total = weights[kind][(*own_view, lane, rows)].astype(F32) + getattr(r, f"sum_{kind}_{part}_0")[...].astype(F32)
            r.attn_sum[16 * part : 16 * part + 16, cols] = total.reshape(16, -1)

    last_step("o", back_o[0], slice(QKV, AW))
    mlp_back_c.wait_recv()

    @pl.when(lends)
    def _():
        r.d_mlp[...] = r.mlp_c[...]

    @pl.when(carries)
    def _():
        r.d_mlp[...] = r.mlp_sum[core]

    last_step("q", back_q[0], slice(0, QKV))
    attn_back = send(r.attn_sum, r.attn_x, "x", "swap_q", gives=x_hi == 1, takes=x_hi == 1)
    gain_add(6, g_step)
    sums = r.gains[...]
    r.d_gain[...] = reorder(sums)
    r.d_gain[0:1] = reorder(sums[0:1] / attn_gain)
    r.d_gain[2:3] = sums[2:3]

    @pl.when(x_hi == 0)
    def _():
        r.d_attn[...] = r.attn_sum[...]

    attn_back.wait_recv()

    @pl.when(x_hi == 1)
    def _():
        r.d_attn[...] = r.attn_x[...]

    flush()


def unpack(*refs):
    layer_in, input_in, d_attn, d_mlp, d_gain = refs[:5]
    (
        layer_out,
        input_grad,
        attn_gain,
        w_query,
        w_key,
        w_value,
        query_gain,
        key_gain,
        w_out,
        mlp_gain,
        w_gate,
        w_up,
        w_down,
    ) = refs[5:18]
    layer_out[...] = layer_in[...]
    input_grad[...] = input_in[...]
    attn_gain[...] = d_gain[0]
    mlp_gain[...] = d_gain[1]
    query_gain[...] = d_gain[2, 0:HEAD]
    key_gain[...] = d_gain[2, HEAD : 2 * HEAD]
    w_query[...] = d_attn[:, 0:256]
    w_key[...] = d_attn[:, 256:384]
    w_value[...] = d_attn[:, 384:512]
    w_out[...] = d_attn[:, 512:768]
    w_gate[...] = d_mlp[:, 0:HID]
    w_up[...] = d_mlp[:, HID : 2 * HID]
    w_down[...] = d_mlp[:, 2 * HID : MW]


def rope_tables():
    position = np.arange(SEQ, dtype=np.float32)[:, None]
    channel = np.arange(HEAD // 2, dtype=np.float32)[None, :]
    rate = np.exp(channel * np.float32(-2.0 * math.log(ROPE_BASE) / HEAD)).astype(np.float32)
    angle = (position * rate).astype(np.float32).astype(np.float64)
    cos = np.cos(angle).astype(np.float32)
    sin = np.sin(angle).astype(np.float32)
    shape = (4, ROWS, HEAD)
    return (
        np.concatenate([cos, cos], axis=1).reshape(shape),
        np.concatenate([-sin, sin], axis=1).reshape(shape),
    )


def body(
    tokens,
    attn_gain,
    w_query,
    key_weight,
    value_weight,
    query_gain,
    key_gain,
    w_out,
    mlp_gain,
    w_gate,
    w_up,
    w_down,
    out_cotangent,
):
    cosf, sinf = rope_tables()
    vmem = pl.BlockSpec(memory_space=pltpu.VMEM)

    def out(*shape):
        return jax.ShapeDtypeStruct(shape, F32)

    packed = pl.pallas_call(
        kernel,
        out_shape=(
            jax.ShapeDtypeStruct((ROWS, WIDTH), BF16),
            out(ROWS, WIDTH),
            out(64, AW),
            out(64, MW),
            out(8, WIDTH),
        ),
        in_specs=[vmem] * len(INPUTS),
        out_specs=(vmem,) * len(OUTPUTS),
        scratch_shapes=[pltpu.VMEM(*SCRATCH[name]) for name in NAMES]
        + [pltpu.SemaphoreType.DMA((N_SEM,)), pltpu.SemaphoreType.DMA((N_SEM,))],
        compiler_params=pltpu.CompilerParams(
            collective_id=0, has_side_effects=True, vmem_limit_bytes=64 * 2**20 - 2**17
        ),
        name="layer",
    )(
        tokens,
        out_cotangent,
        w_query,
        key_weight,
        value_weight,
        w_out.T,
        w_gate,
        w_up,
        w_down.T,
        attn_gain,
        mlp_gain,
        query_gain,
        key_gain,
        jnp.asarray(cosf),
        jnp.asarray(sinf),
    )
    parts = list(pl.pallas_call(
        unpack,
        out_shape=[
            jax.ShapeDtypeStruct((ROWS, WIDTH), BF16),
            out(ROWS, WIDTH),
            out(WIDTH),
            out(64, 256),
            out(64, HEAD),
            out(64, HEAD),
            out(HEAD),
            out(HEAD),
            out(64, 256),
            out(WIDTH),
            out(64, HID),
            out(64, HID),
            out(64, HID),
        ],
        in_specs=[vmem] * 5,
        out_specs=[vmem] * 13,
        name="unpack",
    )(*packed))
    parts[8] = parts[8].T
    parts[12] = parts[12].T
    return tuple(parts)


def solution(mesh):
    rows = P(("dp", "tensor"), None)
    first = P("dp", "tensor")
    second = P("tensor", "dp")
    whole = P()
    return jax.shard_map(
        body,
        mesh=mesh,
        in_specs=(
            rows,
            whole,
            first,
            first,
            first,
            whole,
            whole,
            second,
            whole,
            first,
            first,
            second,
            rows,
        ),
        out_specs=(
            rows,
            rows,
            whole,
            first,
            first,
            first,
            whole,
            whole,
            second,
            whole,
            first,
            first,
            second,
        ),
        check_vma=False,
    )
```

time: 220 us -> 169 us (0.77)
  Pallas kernels: 202 us -> 165 us
  local copies, waits for them, and re-layouts: 12.8 us -> 0 us
    pallas_call x1, Pallas kernels: 202 us -> 163 us  [body(): pl.pallas_call(kernel, out_shape=(jax.ShapeDtypeStruct((ROWS, WIDTH), BF1...]
    transpose x2 -> x0, local copies, waits for them, and re-layouts: 3.23 us -> none  [the longest x1 1.7 us: body(): d_mlp[:, 2 * HID:MW]]
    pallas_call x0 -> x1, Pallas kernels: none -> 2.91 us  [body(): pl.pallas_call(unpack, out_shape=[jax.ShapeDtypeStruct((ROWS, WIDTH), BF1...]
    unnamed x12 -> x0, local copies, waits for them, and re-layouts: 2.86 us -> none
    slice x2 -> x0, local copies, waits for them, and re-layouts: 2.84 us -> none  [the longest x1 1.44 us: body(): d_gain[1]]
    reshape x2 -> x0, local copies, waits for them, and re-layouts: 2.56 us -> none  [the longest x1 1.28 us: body(): attn_gain.reshape(1, -1)]
where the time goes in v2:
time: 169 us; the launch traced here: 166 us
  Pallas kernels  165 us (98%)
    pallas_call x1, Pallas kernels, body(): pl.pallas_call(kernel, out_shape=(jax.ShapeDtypeStruct((ROWS, WIDTH), BF1...  163 us

profile of v2, /device:TPU:8, one launch (start us, length us, event | category | flops | bytes accessed | tf_op | source)
XLA Modules:
  0.0 166.2 jit_solution(10840381529479778954)
XLA Ops:
  0.6 162.5 %layer.1 = (bf16[256,1024]{1,0:T(8,128)(2,1)}, f32[256,1024]{1,0:T(8,128)}, f32[64,768]{1,0:T(8,128)}, f32[64,1152]{1,0:T(8,128)}, f32[8,1024]{1,0:T(8,128)}) custom-call(bf16[256,1024]{1,0:T(8,128)(2,1)} %refs_0_.1, bf16[256,1024]{1,0:T(8,128)(2,1)} %refs_1_.1, bf16[64,256]{1,0:T(8,128)(2,1)} %refs_2_.1, bf16[64,128]{1,0:T(8,128)(2,1)} %refs_3_.1, ...), custom_call_target="tpu_custom_call" | custom-call | tf_op jit(solution)/shard_map/layer/pallas_call | solution.py:941
  163.2 2.9 %unpack.1 = (bf16[256,1024]{1,0:T(8,128)(2,1)}, f32[256,1024]{1,0:T(8,128)}, f32[1024]{0:T(1024)}, f32[64,256]{1,0:T(8,128)}, f32[64,128]{1,0:T(8,128)}, /*index...) custom-call(bf16[256,1024]{1,0:T(8,128)(2,1)} %get-tuple-element.31., ...), custom_call_target="tpu_custom_call" | custom-call | tf_op jit(solution)/shard_map/unpack/pallas_call | solution.py:975

commit v3 on v2

--- a/solution.py
+++ b/solution.py
@@ -58,7 +58,7 @@
     "pack_o": ((64, OW), BF16),
     "pack_m": ((64, MW), BF16),
     "a_full": ((4, ROWS, WIDTH), BF16),
-    "m_full": ((4, ROWS, WIDTH), BF16),
+    "m_full": ((2, 2, 2, 2, 2, 64, 512), BF16),
     "c_full": ((4, ROWS, WIDTH), BF16),
     "d_full": ((4, ROWS, WIDTH), BF16),
     "qkp": ((2, 4, ROWS, 384), F32),
@@ -75,7 +75,6 @@
     "hid": ((2, 4, ROWS, HID), BF16),
     "dgu": ((2, 4, ROWS, 2 * HID), BF16),
     "own": ((ROWS, WIDTH), F32),
-    "own_down": ((ROWS, WIDTH), F32),
     "resid": ((ROWS, WIDTH), F32),
     "stage": ((3, ROWS, WIDTH), BF16),
     "stage_down": ((3, ROWS, WIDTH), BF16),
@@ -87,9 +86,11 @@
     "gain_in": ((7, 8, WIDTH), F32),
     "core_q": ((2, 2, 2, 2, 1, 64, QKV), BF16),
     "core_o": ((2, 2, 2, 2, 1, 64, OW), BF16),
+    "raw": ((2, 2, 64, MW), BF16),
     "mlp_x": ((2, 64, MW), BF16),
     "mlp_c": ((64, MW), F32),
-    "attn_x": ((64, AW), F32),
+    "attn_x": ((64, AW), BF16),
+    "attn_low": ((64, AW), BF16),
     "attn_sum": ((64, AW), F32),
     "mlp_sum": ((2, 64, MW), F32),
 }
@@ -115,8 +116,8 @@
         SCRATCH[f"sum_w_{_part}_{_step}"] = (cube_shape(_part, _step, 2, MW), BF16)
 
 NAMES = list(SCRATCH)
-N_SEM = 107
-INPUTS = ["tok", "cot", "wq", "wk", "wv", "wo", "wg", "wu", "wd", "ag", "mg", "qg", "kg", "cosf", "sinf"]
+N_SEM = 109
+INPUTS = ["tok", "cot", "wq", "wk", "wv", "wo", "wg", "wu", "wd", "ag", "mg", "qg", "kg", "rope"]
 OUTPUTS = ["layer_out", "input_grad", "d_attn", "d_mlp", "d_gain"]
 
 
@@ -175,7 +176,12 @@
         "za": (dp + 4 - 8 * (z % 2), tn),
         "zb": (dp + 4 * (3 - 2 * z), tn),
     }
-    pair = "y"
+    links = list(nbr)
+    pair = "p"
+    nbr["p"] = (dp, tn + jnp.where(core == 0, 2 - 4 * y_lo, 1 - 2 * x_lo))
+    kx = (x_lo + x_hi) % 2
+    lends = (core + x_lo) % 2
+    role = 2 * lends + kx
 
     def square(k):
         kx, ky = k % 2, k // 2
@@ -235,28 +241,29 @@
     lane = pl.ds(core, 1)
     lanes = {"q": lane, "o": lane, "w": both}
     weights = {"q": r.w_q, "o": r.w_o, "w": r.w_m}
+    grads = {"q": r.m_full, "o": r.w_o, "w": r.w_m}
     own_slot = (own_bit["yo"], own_bit["zb"], own_bit["za"], own_bit["xo"])
     own_view = tuple(pl.ds(bit, 1) for bit in own_slot)
 
     def step_key(kind, part, step, back):
         return (kind, part, step, back and kind == "w" and step == 3)
 
-    def gather_step(kind, step):
+    def gather_later(kind, step):
         out = []
         for part in range(4):
             axes = part_axes(part)
             rows = pl.ds(16 * part, 16)
             view = weights[kind].at[(*slots(axes[:step], None, lanes[kind]), rows)]
-            out.append(send(view, view, axes[step], step_key(kind, part, step, False)))
+            out.append(later(view, view, axes[step], step_key(kind, part, step, False)))
         return out
 
-    def core_send(kind, late):
+    def core_later(kind, late):
         out = []
         for part in range(4):
             axes = part_axes(part)
             rows = pl.ds(16 * part, 16)
             view = weights[kind].at[(*slots(axes[:3], axes[3] if late else None, lane), rows)]
-            out.append(send(view, view, "c", ("core", kind, late, part)))
+            out.append(later(view, view, "c", ("core", kind, late, part)))
         return out
 
     def reduce_later(kind, step):
@@ -264,7 +271,7 @@
         for part in range(4):
             axes = part_axes(part)
             rows = pl.ds(16 * part, 16)
-            view = weights[kind].at[(*slots(axes[:step], axes[step], lanes[kind]), rows)]
+            view = grads[kind].at[(*slots(axes[:step], axes[step], lanes[kind]), rows)]
             buf = getattr(r, f"sum_{kind}_{part}_{step}")
             out.append(later(view, buf, axes[step], step_key(kind, part, step, True)))
         return out
@@ -279,15 +286,13 @@
             rows = pl.ds(16 * part, 16)
             index = (*slots(axes[:step], None, lanes[kind]), rows)
             group[part].wait_recv()
-            total = weights[kind][index].astype(F32) + getattr(r, f"sum_{kind}_{part}_{step}")[...].astype(F32)
-            weights[kind][index] = total.astype(BF16)
+            total = grads[kind][index].astype(F32) + getattr(r, f"sum_{kind}_{part}_{step}")[...].astype(F32)
+            grads[kind][index] = total.astype(BF16)
 
     barrier = pltpu.get_barrier_semaphore()
-    for to in nbr:
+    for to in links:
         pl.semaphore_signal(barrier, inc=1, device_id=nbr[to], device_id_type=MESH)
 
-    carries = core == x_lo
-    lends = core != x_lo
     r.pack_q[:, 0:256] = r.wq[...]
     r.pack_q[:, 256:384] = r.wk[...]
     r.pack_q[:, 384:512] = r.wv[...]
@@ -301,9 +306,9 @@
         r.w_q[(*own_view, lane)] = r.pack_q[...].reshape(1, 1, 1, 1, 1, 64, QKV)
         r.w_o[(*own_view, lane)] = r.pack_o[...].reshape(1, 1, 1, 1, 1, 64, OW)
 
-    @pl.when(carries)
+    @pl.when(lends == 0)
     def _():
-        r.w_m[(*own_view, lane)] = r.pack_m[...].reshape(1, 1, 1, 1, 1, 64, MW)
+        r.raw[0, pl.ds(core, 1)] = r.pack_m[...].reshape(1, 64, MW)
 
     attn_gain = reorder(r.ag[...].astype(F32).reshape(1, WIDTH))
     mlp_gain = reorder(r.mg[...].astype(F32).reshape(1, WIDTH))
@@ -316,13 +321,16 @@
     rows_x = rows_in()
     r.a_full[square(0)] = (rows_x * row_scale(rows_x) * attn_gain).astype(BF16)
     r.c_full[group(0)] = reorder(r.cot[...])
-    pl.semaphore_wait(barrier, len(nbr))
-
-    swap_q = send(r.pack_q, r.w_q.at[(*own_slot, core)], "x", "swap_q", gives=x_hi == 1, takes=x_hi == 1)
-    swap_o = send(r.pack_o, r.w_o.at[(*own_slot, core)], "x", "swap_o", gives=x_hi == 1, takes=x_hi == 1)
+    pl.semaphore_wait(barrier, len(links))
+
+    odd = x_hi == 1
+    swap_q = send(r.pack_q, r.w_q.at[(*own_slot, core)], "x", "swap_q", gives=odd, takes=odd)
+    swap_o = send(r.pack_o, r.w_o.at[(*own_slot, core)], "x", "swap_o", gives=odd, takes=odd)
     mlp_pair = r.w_m.at[own_slot]
-    mlp_to_core = send(r.pack_m, r.w_m.at[(*own_slot, core)], "c", "mlp_c", gives=lends, takes=carries)
-    mlp_to_x = later(mlp_pair, mlp_pair, "x", "mlp_x", gives=carries, takes=lends)
+    raw_y = send(r.pack_m, r.raw.at[1, core], "y", "raw_y")
+    raw_c0 = send(r.pack_m, r.raw.at[0, core], "c", "raw_c0", gives=lends == 1, takes=lends == 0)
+    raw_c1 = later(r.raw.at[1, core], r.raw.at[1, core], "c", "raw_c1", gives=lends == 1, takes=lends == 0)
+    mlp_to_x = later(r.raw.at[1 - kx], mlp_pair, "x", "mlp_x", gives=lends == 0, takes=lends == 1)
 
     def square_gather(buf):
         def half(k, n):
@@ -330,10 +338,14 @@
 
         x0 = send(half(0, 0), half(0, 0), "x", "sg_x0")
         y1 = send(half(0, 1), half(0, 1), "y", "sg_y1")
-        x1 = send(half(0, 1), half(0, 1), "x", "sg_x1")
-        y0 = send(half(0, 0), half(0, 0), "y", "sg_y0")
+        x1 = later(half(0, 1), half(0, 1), "x", "sg_x1")
+        y0 = later(half(0, 0), half(0, 0), "y", "sg_y0")
         fy = later(half(1, 0), half(1, 0), "y", "sg_fy")
         fx = later(half(2, 1), half(2, 1), "x", "sg_fx")
+
+        def second():
+            x1.start()
+            y0.start()
 
         def forward():
             x0.wait_recv()
@@ -341,37 +353,45 @@
             y1.wait_recv()
             fx.start()
 
-        return forward, x1, y0, [fx, fy]
-
-    a_forward, a_x1, a_y0, a_far = square_gather(r.a_full)
+        return second, forward, x1, y0, [fx, fy]
+
+    a_second, a_forward, a_x1, a_y0, a_far = square_gather(r.a_full)
+    gather = {kind: [gather_later(kind, step) for step in range(4)] for kind in "qow"}
+    to_core = {kind: [core_later(kind, late) for late in (False, True)] for kind in "qo"}
+
+    def advance(kind, step):
+        wait_recv(gather[kind][step - 1])
+        start(gather[kind][step])
 
     swap_q.wait_recv()
-    step_q = gather_step("q", 0)
-    wait_recv(step_q)
-    step_q = gather_step("q", 1)
+    start(gather["q"][0])
+    raw_y.wait_recv()
+    raw_c1.start()
     swap_o.wait_recv()
-    step_o = gather_step("o", 0)
-    mlp_to_core.wait_recv()
+    advance("q", 1)
+    start(gather["o"][0])
+    raw_c0.wait_recv()
+    raw_c1.wait_recv()
     mlp_to_x.start()
+    advance("q", 2)
     a_forward()
-    wait_recv(step_q)
-    step_q = gather_step("q", 2)
-    wait_recv(step_o)
-    step_o = gather_step("o", 1)
-    wait_recv(step_q)
-    step_q = gather_step("q", 3)
-    early = core_send("q", False)
-    wait_recv(step_o)
-    step_o = gather_step("o", 2)
+
+    @pl.when(lends == 0)
+    def _():
+        r.w_m[own_view] = r.raw[pl.ds(kx, 1)].reshape(1, 1, 1, 1, 2, 64, MW)
+
+    advance("q", 3)
+    start(to_core["q"][0])
+    advance("o", 1)
     mlp_to_x.wait_recv()
-    step_w = gather_step("w", 0)
-    wait_recv(step_q)
-    late = core_send("q", True)
-    wait_recv(step_o)
-    step_o = gather_step("o", 3)
-    early_o = core_send("o", False)
-    wait_recv(early)
-    wait_recv(late)
+    start(gather["w"][0])
+    a_second()
+    wait_recv(gather["q"][3])
+    start(to_core["q"][1])
+    advance("o", 2)
+    advance("w", 1)
+    wait_recv(to_core["q"][0])
+    wait_recv(to_core["q"][1])
 
     def w_qkv(g):
         return r.w_q[g].reshape(WIDTH, QKV)
@@ -388,20 +408,36 @@
     c_pair = later(r.c_full.at[group(0)], r.c_full.at[core + 2], pair, "cot_p")
     c_core = later(r.c_full.at[group(0)], r.c_full.at[group(0)], "c", "cot_c")
 
+    first_half = lax.broadcasted_iota(jnp.int32, (ROWS, HEAD), 1) < HEAD // 2
+
+    def turns(blk):
+        table = r.rope[blk]
+        swapped = pltpu.roll(table, 64, 1)
+        return jnp.where(first_half, table, swapped), jnp.where(first_half, -swapped, table)
+
     def qkv_block(k, carry):
-        at(k, 1, a_x1.wait_recv)
-        at(k, 2, a_y0.wait_recv)
+        @pl.when(k == 1)
+        def _():
+            a_x1.wait_recv()
+            c_pair.start()
+            c_core.start()
+            advance("o", 3)
+            start(to_core["o"][0])
+
+        @pl.when(k == 2)
+        def _():
+            a_y0.wait_recv()
+            advance("w", 2)
 
         @pl.when(k == 3)
         def _():
             wait_recv(a_far)
-            c_pair.start()
-            c_core.start()
+            wait_recv(gather["o"][3])
+            start(to_core["o"][1])
 
         blk = square(k)
         rows = r.a_full[blk]
-        cos = r.cosf[blk]
-        sin = r.sinf[blk]
+        cos, sin = turns(blk)
         for g in range(2):
             acc = dot_nn(rows, w_qkv(g))
             r.qkp[g, blk] = acc[:, :384]
@@ -420,10 +456,6 @@
         return carry
 
     lax.fori_loop(0, 4, qkv_block, 0)
-    wait_recv(step_w)
-    step_w = gather_step("w", 1)
-    wait_recv(step_o)
-    late_o = core_send("o", True)
 
     key_at = lax.broadcasted_iota(jnp.int32, (ROWS, 512), 0)
     query_at = lax.broadcasted_iota(jnp.int32, (ROWS, 512), 1) % ROWS
@@ -494,49 +526,49 @@
                 d0.start()
                 d1.start()
 
-            at(n, 1, x0.start)
-            at(n, 2, y1.start)
+            at(n, 2, x0.start)
+            at(n, 3, y1.start)
             return carry
 
         lax.fori_loop(0, 4, block, 0)
-        d1.wait_recv()
-        r.stage[0, 128:256] = (r.stage[0, 128:256].astype(F32) + r.far[1].astype(F32)).astype(BF16)
-        x1.start()
-        d0.wait_recv()
-        r.stage[1, 0:128] = (r.stage[1, 0:128].astype(F32) + r.far[0].astype(F32)).astype(BF16)
-        y0.start()
+
+        def relay():
+            d1.wait_recv()
+            r.stage[0, 128:256] = (r.stage[0, 128:256].astype(F32) + r.far[1].astype(F32)).astype(BF16)
+            x1.start()
+            d0.wait_recv()
+            r.stage[1, 0:128] = (r.stage[1, 0:128].astype(F32) + r.far[0].astype(F32)).astype(BF16)
+            y0.start()
 
         def finish():
             wait_recv([x0, y1, x1, y0])
             return r.own[...] + r.near[0].astype(F32) + r.near[1].astype(F32)
 
-        return finish
+        return relay, finish
 
     def attend_and_part(blk):
         attend_block(blk)
         return part_o(blk)
 
-    wait_recv(early_o)
-    wait_recv(late_o)
-    wait_recv(step_w)
-    step_w = gather_step("w", 2)
-    o_finish = square_sum(attend_and_part, {})
-    wait_recv(step_w)
-    step_w = gather_step("w", 3)
+    wait_recv(to_core["o"][0])
+    wait_recv(to_core["o"][1])
+    o_relay, o_finish = square_sum(attend_and_part, {3: lambda: advance("w", 3)})
+    o_relay()
     c_pair.wait_recv()
     c_forward = send(r.c_full.at[core + 2], r.c_full.at[core + 2], "c", "cot_f")
     resid = rows_in() + o_finish()
     r.resid[...] = resid
-
-    r.m_full[group(0)] = (resid * row_scale(resid) * mlp_gain).astype(BF16)
+    normed = (resid * row_scale(resid) * mlp_gain).astype(BF16)
+    for half in range(2):
+        r.m_full[0, pl.ds(core, 1), half] = normed[:, 512 * half : 512 * half + 512].reshape(1, 2, 2, 64, 512)
     m_pair = []
     m_forward = []
     for n in range(2):
-        rows = pl.ds(128 * n, 128)
-        m_pair.append(send(r.m_full.at[group(0), rows], r.m_full.at[core + 2, rows], pair, ("m_p", n)))
-        m_forward.append(later(r.m_full.at[core + 2, rows], r.m_full.at[core + 2, rows], "c", ("m_f", n)))
-    m_core = send(r.m_full.at[group(0)], r.m_full.at[group(0)], "c", "m_c")
-    wait_recv(step_w)
+        near_rows, far_rows = (r.m_full.at[place, core, :, n] for place in range(2))
+        m_pair.append(send(near_rows, far_rows, pair, ("m_p", n)))
+        m_forward.append(later(far_rows, far_rows, "c", ("m_f", n)))
+    m_core = send(r.m_full.at[0, core], r.m_full.at[0, core], "c", "m_c")
+    wait_recv(gather["w"][3])
     wait_recv([c_core, c_forward])
 
     def mlp_block(k, carry):
@@ -553,7 +585,7 @@
             wait_recv(m_forward)
 
         i = group(k)
-        rows = r.m_full[i]
+        rows = jnp.concatenate([r.m_full[i // 2, i % 2, half].reshape(ROWS, 512) for half in range(2)], axis=1)
         cots = r.c_full[i]
         for g in range(2):
             pre = dot_nn(rows, w_gu(g))
@@ -597,7 +629,7 @@
 
             @pl.when(n == 3)
             def _():
-                own[...] = acc
+                own[...] = own[...] + acc if hold else acc
 
             return carry
 
@@ -616,12 +648,13 @@
         return dot_nt(r.hid[0, i], w_dn(0)) + dot_nt(r.hid[1, i], w_dn(1))
 
     dm_finish, _ = pair_sum(part_dm, r.stage, r.sum_m, r.own, "dm", False)
-    down_finish, down_pair = pair_sum(part_down, r.stage_down, r.sum_d, r.own_down, "down", True)
-    r.own_down[...] += r.resid[...]
-
+
+    r.input_grad[...] = r.resid[...]
+    down_finish, down_pair = pair_sum(part_down, r.stage_down, r.sum_d, r.input_grad, "down", True)
     def mlp_grads(p, carry):
         cols = pl.ds(pl.multiple_of(256 * p, 256), 256)
-        rows_t = r.m_full[:, :, cols].reshape(SEQ, 256)
+        half_cols = pl.ds(pl.multiple_of(256 * (p % 2), 256), 256)
+        rows_t = r.m_full[:, :, p // 2, :, :, :, half_cols].reshape(SEQ, 256)
         cots_t = r.c_full[:, :, cols].reshape(SEQ, 256)
         for g in range(2):
             grad_gu = dot_tn(rows_t, r.dgu[g].reshape(SEQ, 2 * HID))
@@ -630,9 +663,8 @@
             r.w_m[g, p // 2, p % 2, :, :, :, 2 * HID : MW] = grad_dn.reshape(2, 2, 64, HID).astype(BF16)
         return carry
 
-    lax.fori_loop(0, 4, mlp_grads, 0)
+    lax.fori_loop(0, 2, mlp_grads, 0)
     back_w = {step: reduce_later("w", step) for step in range(4)}
-    start(back_w[3])
 
     dm = dm_finish()
     resid = r.resid[...]
@@ -644,7 +676,10 @@
     dresid = reorder(r.cot[...].astype(F32)) + inv_m * scaled - resid * (inv_m * inv_m * inv_m * inner)
     r.resid[...] = dresid
     r.d_full[square(0)] = dresid.astype(BF16)
-    d_forward, d_x1, d_y0, d_far = square_gather(r.d_full)
+    d_second, d_forward, d_x1, d_y0, d_far = square_gather(r.d_full)
+    lax.fori_loop(2, 4, mlp_grads, 0)
+    start(back_w[3])
+    d_second()
     r.dk[...] = jnp.zeros((2, 4, ROWS, HEAD), F32)
     r.dv[...] = jnp.zeros((2, 4, ROWS, HEAD), F32)
 
@@ -667,24 +702,25 @@
         return back.astype(BF16), jnp.sum(grad * hat, axis=0, keepdims=True)
 
     def turn_back(grad, blk):
-        return grad * r.cosf[blk] - pltpu.roll(grad, 64, 1) * r.sinf[blk]
+        cos, sin = turns(blk)
+        return grad * cos - pltpu.roll(grad, 64, 1) * sin
 
     def back_block(k, gain_sum):
         @pl.when(k == 1)
         def _():
             d_forward()
-            down_pair.start()
             d_x1.wait_recv()
+
+        @pl.when(k == 2)
+        def _():
+            d_y0.wait_recv()
             reduce_add("w", 3, back_w[3])
             start(back_w[2])
-
-        at(k, 2, d_y0.wait_recv)
 
         @pl.when(k == 3)
         def _():
             wait_recv(d_far)
-            reduce_add("w", 2, back_w[2])
-            start(back_w[1])
+            down_pair.start()
 
         i = square(k)
         rows = r.d_full[i]
@@ -714,6 +750,33 @@
     other = pl.ds(flip(core), 1)
     whole = (both, both, both, both)
 
+    def core_sum(kind, buf, copy):
+        copy.wait_recv()
+        index = (*whole, lane)
+        total = grads[kind][index].astype(F32) + buf[...].astype(F32)
+        grads[kind][index] = total.astype(BF16)
+
+    def key_block(j, gain_sum):
+        for g in range(2):
+            grad = turn_back(r.dk[g, j] * SCORE_SCALE, j)
+            low, part = unnorm(r.qkp[g, j, :, 256:384], key_gain, grad)
+            r.dgu[g, j, :, 256:384] = low
+            r.dgu[g, j, :, 384:512] = r.dv[g, j].astype(BF16)
+            gain_sum = gain_sum + part
+        return gain_sum
+
+    k_gain_part = lax.fori_loop(0, 4, key_block, jnp.zeros((1, HEAD), F32))
+    r.gains[2:3, 0:HEAD] = q_gain_part
+    r.gains[2:3, HEAD : 2 * HEAD] = k_gain_part
+
+    def qkv_grads(p, carry):
+        cols = pl.ds(pl.multiple_of(256 * p, 256), 256)
+        rows_t = r.a_full[:, :, cols].reshape(SEQ, 256)
+        for g in range(2):
+            grad = dot_tn(rows_t, r.dgu[g, :, :, 0:QKV].reshape(SEQ, QKV))
+            r.m_full[g, p // 2, p % 2] = grad.reshape(2, 2, 64, QKV).astype(BF16)
+        return carry
+
     def out_grads(p, carry):
         cols = pl.ds(pl.multiple_of(256 * p, 256), 256)
         grads_t = r.d_full[:, :, cols].reshape(SEQ, 256)
@@ -725,27 +788,12 @@
             r.w_o[g, p // 2, p % 2] = dot_tn(grads_t, mixed).reshape(2, 2, 64, OW).astype(BF16)
         return carry
 
-    def core_sum(kind, buf, copy):
-        copy.wait_recv()
-        index = (*whole, lane)
-        total = weights[kind][index].astype(F32) + buf[...].astype(F32)
-        weights[kind][index] = total.astype(BF16)
-
+    lax.fori_loop(0, 4, qkv_grads, 0)
+    q_core = send(r.m_full.at[(*whole, other)], r.core_q, "c", "q_core")
     lax.fori_loop(0, 4, out_grads, 0)
     o_core = send(r.w_o.at[(*whole, other)], r.core_o, "c", "o_core")
-
-    def key_block(j, gain_sum):
-        for g in range(2):
-            grad = turn_back(r.dk[g, j] * SCORE_SCALE, j)
-            low, part = unnorm(r.qkp[g, j, :, 256:384], key_gain, grad)
-            r.dgu[g, j, :, 256:384] = low
-            r.dgu[g, j, :, 384:512] = r.dv[g, j].astype(BF16)
-            gain_sum = gain_sum + part
-        return gain_sum
-
-    k_gain_part = lax.fori_loop(0, 4, key_block, jnp.zeros((1, HEAD), F32))
-    r.gains[2:3, 0:HEAD] = q_gain_part
-    r.gains[2:3, HEAD : 2 * HEAD] = k_gain_part
+    reduce_add("w", 2, back_w[2])
+    start(back_w[1])
     flush()
 
     def part_da(blk):
@@ -756,118 +804,119 @@
     back_o = {step: reduce_later("o", step) for step in range(4)}
     back_q = {step: reduce_later("q", step) for step in range(4)}
 
+    def tail_q():
+        core_sum("q", r.core_q, q_core)
+        start(back_q[3])
+
     def tail_o():
         core_sum("o", r.core_o, o_core)
         start(back_o[3])
 
-    def tail_w():
-        reduce_add("w", 1, back_w[1])
-        start(back_w[0])
-
-    a_finish = square_sum(part_da, {1: tail_o, 2: tail_w})
-
-    def qkv_grads(p, carry):
-        cols = pl.ds(pl.multiple_of(256 * p, 256), 256)
-        rows_t = r.a_full[:, :, cols].reshape(SEQ, 256)
-        for g in range(2):
-            grad = dot_tn(rows_t, r.dgu[g, :, :, 0:QKV].reshape(SEQ, QKV))
-            r.w_q[g, p // 2, p % 2] = grad.reshape(2, 2, 64, QKV).astype(BF16)
-        return carry
-
-    links = ["c", "za", "zb", "yo", "xo", "y", "x"]
+    a_relay, a_finish = square_sum(part_da, {1: tail_q, 3: tail_o})
+
+    gain_links = ["c", "za", "zb", "yo", "xo", "y", "x"]
 
     def gain_send(n):
-        return send(r.gains, r.gain_in.at[n], links[n], ("gain", n))
+        return send(r.gains, r.gain_in.at[n], gain_links[n], ("gain", n))
 
     def gain_add(n, copy):
         copy.wait_send()
         copy.wait_recv()
         r.gains[...] += r.gain_in[n]
 
+    sum_pair = r.w_m.at[own_slot]
+    back_x = later(sum_pair, r.mlp_x, "x", "mlp_x", gives=lends == 1, takes=lends == 0)
+    back_y0 = later(r.mlp_x, r.raw.at[0], "y", "raw_y", gives=role == 0, takes=role == 0)
+    back_y1 = later(sum_pair, r.raw.at[0], "y", "raw_y", gives=role == 1, takes=role == 1)
+    mlp_back_c = later(r.mlp_sum.at[flip(core)], r.mlp_c, "c", "raw_c0", gives=lends == 0, takes=lends == 1)
+
+    def reduce_next(kind, step, back):
+        reduce_add(kind, step, back[step])
+        start(back[step - 1])
+
     g_step = gain_send(0)
-    lax.fori_loop(0, 4, qkv_grads, 0)
-    q_core = send(r.w_q.at[(*whole, other)], r.core_q, "c", "q_core")
+    reduce_next("w", 1, back_w)
     gain_add(0, g_step)
     g_step = gain_send(1)
-    reduce_add("o", 3, back_o[3])
-    start(back_o[2])
-    core_sum("q", r.core_q, q_core)
-    start(back_q[3])
+    reduce_next("q", 3, back_q)
+    a_relay()
+    reduce_next("o", 3, back_o)
     gain_add(1, g_step)
     g_step = gain_send(2)
-    mlp_back_x = later(mlp_pair, r.mlp_x, "x", "mlp_x", gives=lends, takes=carries)
-    mlp_back_c = later(r.mlp_sum.at[flip(core)], r.mlp_c, "c", "mlp_c", gives=carries, takes=lends)
     reduce_add("w", 0, back_w[0])
-    mlp_back_x.start()
-    reduce_add("o", 2, back_o[2])
-    start(back_o[1])
+    back_x.start()
+    back_y1.start()
     r.layer_out[...] = reorder(down_finish()).astype(BF16)
+    reduce_next("q", 2, back_q)
+    reduce_next("o", 2, back_o)
     gain_add(2, g_step)
     g_step = gain_send(3)
-    reduce_add("q", 3, back_q[3])
-    start(back_q[2])
-    reduce_add("o", 1, back_o[1])
-    start(back_o[0])
+    back_x.wait_recv()
+    back_y0.start()
+    reduce_next("q", 1, back_q)
+    reduce_next("o", 1, back_o)
     gain_add(3, g_step)
     g_step = gain_send(4)
-    reduce_add("q", 2, back_q[2])
-    start(back_q[1])
-    mlp_back_x.wait_recv()
-
-    @pl.when(carries)
-    def _():
-        r.mlp_sum[...] = mlp_pair[...].astype(F32) + r.mlp_x[...].astype(F32)
-
-    mlp_back_c.start()
-    gain_add(4, g_step)
-
-    rows_x = rows_in()
-    inv_a = row_scale(rows_x)
-    scaled = a_finish() * attn_gain
-    g_step = gain_send(5)
-    inner = jnp.mean(scaled * rows_x, axis=-1, keepdims=True)
-    r.input_grad[...] = reorder(r.resid[...] + inv_a * scaled - rows_x * (inv_a * inv_a * inv_a * inner))
-    reduce_add("q", 1, back_q[1])
-    start(back_q[0])
-    gain_add(5, g_step)
-    g_step = gain_send(6)
 
     def last_step(kind, group, cols):
         for part in range(4):
             rows = pl.ds(16 * part, 16)
             group[part].wait_recv()
-            total = weights[kind][(*own_view, lane, rows)].astype(F32) + getattr(r, f"sum_{kind}_{part}_0")[...].astype(F32)
+            total = grads[kind][(*own_view, lane, rows)].astype(F32) + getattr(r, f"sum_{kind}_{part}_0")[...].astype(F32)
             r.attn_sum[16 * part : 16 * part + 16, cols] = total.reshape(16, -1)
+        r.attn_low[:, cols] = r.attn_sum[:, cols].astype(BF16)
 
     last_step("o", back_o[0], slice(QKV, AW))
+    last_step("q", back_q[0], slice(0, QKV))
+    attn_back = send(r.attn_low, r.attn_x, "x", "swap_q", gives=odd, takes=odd)
+    gain_add(4, g_step)
+    g_step = gain_send(5)
+
+    rows_x = rows_in()
+    inv_a = row_scale(rows_x)
+    scaled = a_finish() * attn_gain
+    inner = jnp.mean(scaled * rows_x, axis=-1, keepdims=True)
+    r.input_grad[...] = reorder(r.resid[...] + inv_a * scaled - rows_x * (inv_a * inv_a * inv_a * inner))
+    gain_add(5, g_step)
+    g_step = gain_send(6)
+    back_y0.wait_recv()
+    back_y1.wait_recv()
+
+    @pl.when(role == 0)
+    def _():
+        r.mlp_sum[...] = sum_pair[...].astype(F32) + r.raw[0].astype(F32)
+
+    @pl.when(role == 1)
+    def _():
+        r.mlp_sum[...] = r.mlp_x[...].astype(F32) + r.raw[0].astype(F32)
+
+    mlp_back_c.start()
+
+    @pl.when(lends == 0)
+    def _():
+        r.d_mlp[...] = r.mlp_sum[core]
+
+    @pl.when(x_hi == 0)
+    def _():
+        r.d_attn[...] = r.attn_sum[...]
+
+    attn_back.wait_recv()
+
+    @pl.when(odd)
+    def _():
+        r.d_attn[...] = r.attn_x[...].astype(F32)
+
     mlp_back_c.wait_recv()
 
-    @pl.when(lends)
+    @pl.when(lends == 1)
     def _():
         r.d_mlp[...] = r.mlp_c[...]
 
-    @pl.when(carries)
-    def _():
-        r.d_mlp[...] = r.mlp_sum[core]
-
-    last_step("q", back_q[0], slice(0, QKV))
-    attn_back = send(r.attn_sum, r.attn_x, "x", "swap_q", gives=x_hi == 1, takes=x_hi == 1)
     gain_add(6, g_step)
     sums = r.gains[...]
     r.d_gain[...] = reorder(sums)
     r.d_gain[0:1] = reorder(sums[0:1] / attn_gain)
     r.d_gain[2:3] = sums[2:3]
-
-    @pl.when(x_hi == 0)
-    def _():
-        r.d_attn[...] = r.attn_sum[...]
-
-    attn_back.wait_recv()
-
-    @pl.when(x_hi == 1)
-    def _():
-        r.d_attn[...] = r.attn_x[...]
-
     flush()
 
 
@@ -903,18 +952,14 @@
     w_down[...] = d_mlp[:, 2 * HID : MW]
 
 
-def rope_tables():
+def rope_table():
     position = np.arange(SEQ, dtype=np.float32)[:, None]
     channel = np.arange(HEAD // 2, dtype=np.float32)[None, :]
     rate = np.exp(channel * np.float32(-2.0 * math.log(ROPE_BASE) / HEAD)).astype(np.float32)
     angle = (position * rate).astype(np.float32).astype(np.float64)
     cos = np.cos(angle).astype(np.float32)
     sin = np.sin(angle).astype(np.float32)
-    shape = (4, ROWS, HEAD)
-    return (
-        np.concatenate([cos, cos], axis=1).reshape(shape),
-        np.concatenate([-sin, sin], axis=1).reshape(shape),
-    )
+    return np.concatenate([cos, sin], axis=1).reshape(4, ROWS, HEAD)
 
 
 def body(
@@ -932,7 +977,6 @@
     w_down,
     out_cotangent,
 ):
-    cosf, sinf = rope_tables()
     vmem = pl.BlockSpec(memory_space=pltpu.VMEM)
 
     def out(*shape):
@@ -969,8 +1013,7 @@
         mlp_gain,
         query_gain,
         key_gain,
-        jnp.asarray(cosf),
-        jnp.asarray(sinf),
+        jnp.asarray(rope_table()),
     )
     parts = list(pl.pallas_call(
         unpack,

time: 169 us -> 160 us (0.947); the launches traced: 166 us -> 160 us
  Pallas kernels: 165 us -> 159 us
    pallas_call x1, Pallas kernels: 163 us -> 157 us  [body(): pl.pallas_call(kernel, out_shape=(jax.ShapeDtypeStruct((ROWS, WIDTH), BF1...]
where the time goes in v3:
time: 160 us
  Pallas kernels  159 us (99%)
    pallas_call x1, Pallas kernels, body(): pl.pallas_call(kernel, out_shape=(jax.ShapeDtypeStruct((ROWS, WIDTH), BF1...  157 us

profile of v3, /device:TPU:8, one launch (start us, length us, event | category | flops | bytes accessed | tf_op | source)
XLA Modules:
  0.0 160.2 jit_solution(12141430304367917202)
XLA Ops:
  0.6 156.5 %layer.1 = (bf16[256,1024]{1,0:T(8,128)(2,1)}, f32[256,1024]{1,0:T(8,128)}, f32[64,768]{1,0:T(8,128)}, f32[64,1152]{1,0:T(8,128)}, f32[8,1024]{1,0:T(8,128)}) custom-call(bf16[256,1024]{1,0:T(8,128)(2,1)} %refs_0_.1, bf16[256,1024]{1,0:T(8,128)(2,1)} %refs_1_.1, bf16[64,256]{1,0:T(8,128)(2,1)} %refs_2_.1, bf16[64,128]{1,0:T(8,128)(2,1)} %refs_3_.1, ...), custom_call_target="tpu_custom_call" | custom-call | tf_op jit(solution)/shard_map/layer/pallas_call | solution.py:985
  157.2 2.9 %unpack.1 = (bf16[256,1024]{1,0:T(8,128)(2,1)}, f32[256,1024]{1,0:T(8,128)}, f32[1024]{0:T(1024)}, f32[64,256]{1,0:T(8,128)}, f32[64,128]{1,0:T(8,128)}, /*index...) custom-call(bf16[256,1024]{1,0:T(8,128)(2,1)} %get-tuple-element.31., ...), custom_call_target="tpu_custom_call" | custom-call | tf_op jit(solution)/shard_map/unpack/pallas_call | solution.py:1018

commit v4 on v3

--- a/solution.py
+++ b/solution.py
@@ -77,7 +77,7 @@
     "own": ((ROWS, WIDTH), F32),
     "resid": ((ROWS, WIDTH), F32),
     "stage": ((3, ROWS, WIDTH), BF16),
-    "stage_down": ((3, ROWS, WIDTH), BF16),
+    "w_dn": ((2, WIDTH, HID), BF16),
     "far": ((2, 128, WIDTH), BF16),
     "near": ((2, ROWS, WIDTH), BF16),
     "sum_m": ((3, ROWS, WIDTH), BF16),
@@ -374,6 +374,7 @@
     raw_c1.wait_recv()
     mlp_to_x.start()
     advance("q", 2)
+    advance("o", 1)
     a_forward()
 
     @pl.when(lends == 0)
@@ -382,13 +383,14 @@
 
     advance("q", 3)
     start(to_core["q"][0])
-    advance("o", 1)
+    advance("o", 2)
     mlp_to_x.wait_recv()
     start(gather["w"][0])
     a_second()
     wait_recv(gather["q"][3])
     start(to_core["q"][1])
-    advance("o", 2)
+    advance("o", 3)
+    start(to_core["o"][0])
     advance("w", 1)
     wait_recv(to_core["q"][0])
     wait_recv(to_core["q"][1])
@@ -403,7 +405,7 @@
         return r.w_m[g, :, :, :, :, :, 0 : 2 * HID].reshape(WIDTH, 2 * HID)
 
     def w_dn(g):
-        return r.w_m[g, :, :, :, :, :, 2 * HID : MW].reshape(WIDTH, HID)
+        return r.w_dn[g]
 
     c_pair = later(r.c_full.at[group(0)], r.c_full.at[core + 2], pair, "cot_p")
     c_core = later(r.c_full.at[group(0)], r.c_full.at[group(0)], "c", "cot_c")
@@ -421,19 +423,17 @@
             a_x1.wait_recv()
             c_pair.start()
             c_core.start()
-            advance("o", 3)
-            start(to_core["o"][0])
 
         @pl.when(k == 2)
         def _():
             a_y0.wait_recv()
+            wait_recv(gather["o"][3])
+            start(to_core["o"][1])
             advance("w", 2)
 
         @pl.when(k == 3)
         def _():
             wait_recv(a_far)
-            wait_recv(gather["o"][3])
-            start(to_core["o"][1])
 
         blk = square(k)
         rows = r.a_full[blk]
@@ -548,10 +548,14 @@
 
     def attend_and_part(blk):
         attend_block(blk)
+
+        @pl.when(blk == square(3))
+        def _():
+            wait_recv(to_core["o"][0])
+            wait_recv(to_core["o"][1])
+
         return part_o(blk)
 
-    wait_recv(to_core["o"][0])
-    wait_recv(to_core["o"][1])
     o_relay, o_finish = square_sum(attend_and_part, {3: lambda: advance("w", 3)})
     o_relay()
     c_pair.wait_recv()
@@ -569,6 +573,7 @@
         m_forward.append(later(far_rows, far_rows, "c", ("m_f", n)))
     m_core = send(r.m_full.at[0, core], r.m_full.at[0, core], "c", "m_c")
     wait_recv(gather["w"][3])
+    r.w_dn[...] = r.w_m[:, :, :, :, :, :, 2 * HID : MW].reshape(2, WIDTH, HID)
     wait_recv([c_core, c_forward])
 
     def mlp_block(k, carry):
@@ -599,47 +604,43 @@
             r.dgu[g, i, :, HID : 2 * HID] = (grad * act).astype(BF16)
         return carry
 
-    lax.fori_loop(0, 4, mlp_block, 0)
-    flush()
-
-    def pair_sum(part_of, stage, recv, own, name, hold):
+    def pair_sum(part_of, recv, own, name, hold):
+        stage = r.stage
         s3 = later(stage.at[2], recv.at[0], "c", (name, 3))
         s1 = later(stage.at[0], recv.at[1], "c", (name, 1))
         s2 = later(stage.at[1], recv.at[2], pair, (name, 2))
 
         def block(n, carry):
-            acc = part_of(group(3 - n))
+            acc = part_of(group(n + (n // 2) * (5 - 2 * n)))
 
             @pl.when(n == 0)
+            def _():
+                own[...] = own[...] + acc if hold else acc
+
+            @pl.when(n == 1)
+            def _():
+                stage[0] = acc.astype(BF16)
+                s1.start()
+
+            @pl.when(n == 2)
             def _():
                 stage[2] = acc.astype(BF16)
                 s3.start()
 
-            @pl.when(n == 1)
+            @pl.when(n == 3)
             def _():
                 s3.wait_recv()
                 stage[1] = (acc + recv[0].astype(F32)).astype(BF16)
                 if not hold:
                     s2.start()
 
-            @pl.when(n == 2)
-            def _():
-                stage[0] = acc.astype(BF16)
-                s1.start()
-
-            @pl.when(n == 3)
-            def _():
-                own[...] = own[...] + acc if hold else acc
-
             return carry
-
-        lax.fori_loop(0, 4, block, 0)
 
         def finish():
             wait_recv([s1, s2])
             return own[...] + recv[1].astype(F32) + recv[2].astype(F32)
 
-        return finish, s2
+        return block, finish, s2
 
     def part_dm(i):
         return dot_nt(r.dgu[0, i], w_gu(0)) + dot_nt(r.dgu[1, i], w_gu(1))
@@ -647,10 +648,13 @@
     def part_down(i):
         return dot_nt(r.hid[0, i], w_dn(0)) + dot_nt(r.hid[1, i], w_dn(1))
 
-    dm_finish, _ = pair_sum(part_dm, r.stage, r.sum_m, r.own, "dm", False)
-
-    r.input_grad[...] = r.resid[...]
-    down_finish, down_pair = pair_sum(part_down, r.stage_down, r.sum_d, r.input_grad, "down", True)
+    dm_block, dm_finish, _ = pair_sum(part_dm, r.sum_m, r.own, "dm", False)
+    flush()
+    lax.fori_loop(0, 2, mlp_block, 0)
+    lax.fori_loop(0, 2, dm_block, 0)
+    lax.fori_loop(2, 4, mlp_block, 0)
+    lax.fori_loop(2, 4, dm_block, 0)
+
     def mlp_grads(p, carry):
         cols = pl.ds(pl.multiple_of(256 * p, 256), 256)
         half_cols = pl.ds(pl.multiple_of(256 * (p % 2), 256), 256)
@@ -663,8 +667,10 @@
             r.w_m[g, p // 2, p % 2, :, :, :, 2 * HID : MW] = grad_dn.reshape(2, 2, 64, HID).astype(BF16)
         return carry
 
-    lax.fori_loop(0, 2, mlp_grads, 0)
+    lax.fori_loop(0, 4, mlp_grads, 0)
     back_w = {step: reduce_later("w", step) for step in range(4)}
+    flush()
+    start(back_w[3])
 
     dm = dm_finish()
     resid = r.resid[...]
@@ -674,11 +680,12 @@
     r.gains[...] = jnp.zeros((8, WIDTH), F32)
     r.gains[1:2] = jnp.sum(dm * resid * inv_m, axis=0, keepdims=True)
     dresid = reorder(r.cot[...].astype(F32)) + inv_m * scaled - resid * (inv_m * inv_m * inv_m * inner)
+    r.input_grad[...] = resid
     r.resid[...] = dresid
     r.d_full[square(0)] = dresid.astype(BF16)
     d_second, d_forward, d_x1, d_y0, d_far = square_gather(r.d_full)
-    lax.fori_loop(2, 4, mlp_grads, 0)
-    start(back_w[3])
+    down_block, down_finish, down_pair = pair_sum(part_down, r.sum_d, r.input_grad, "down", True)
+    lax.fori_loop(0, 4, down_block, 0)
     d_second()
     r.dk[...] = jnp.zeros((2, 4, ROWS, HEAD), F32)
     r.dv[...] = jnp.zeros((2, 4, ROWS, HEAD), F32)
@@ -756,6 +763,21 @@
         total = grads[kind][index].astype(F32) + buf[...].astype(F32)
         grads[kind][index] = total.astype(BF16)
 
+    def out_grads(p, carry):
+        cols = pl.ds(pl.multiple_of(256 * p, 256), 256)
+        grads_t = r.d_full[:, :, cols].reshape(SEQ, 256)
+        for g in range(2):
+            heads = r.os[g]
+            mixed = jnp.concatenate(
+                [heads[:, :ROWS].reshape(SEQ, HEAD), heads[:, ROWS:].reshape(SEQ, HEAD)], axis=1
+            )
+            r.w_o[g, p // 2, p % 2] = dot_tn(grads_t, mixed).reshape(2, 2, 64, OW).astype(BF16)
+        return carry
+
+    reduce_add("w", 2, back_w[2])
+    start(back_w[1])
+    lax.fori_loop(0, 4, out_grads, 0)
+    o_core = send(r.w_o.at[(*whole, other)], r.core_o, "c", "o_core")
     def key_block(j, gain_sum):
         for g in range(2):
             grad = turn_back(r.dk[g, j] * SCORE_SCALE, j)
@@ -777,59 +799,44 @@
             r.m_full[g, p // 2, p % 2] = grad.reshape(2, 2, 64, QKV).astype(BF16)
         return carry
 
-    def out_grads(p, carry):
-        cols = pl.ds(pl.multiple_of(256 * p, 256), 256)
-        grads_t = r.d_full[:, :, cols].reshape(SEQ, 256)
-        for g in range(2):
-            heads = r.os[g]
-            mixed = jnp.concatenate(
-                [heads[:, :ROWS].reshape(SEQ, HEAD), heads[:, ROWS:].reshape(SEQ, HEAD)], axis=1
-            )
-            r.w_o[g, p // 2, p % 2] = dot_tn(grads_t, mixed).reshape(2, 2, 64, OW).astype(BF16)
-        return carry
-
-    lax.fori_loop(0, 4, qkv_grads, 0)
-    q_core = send(r.m_full.at[(*whole, other)], r.core_q, "c", "q_core")
-    lax.fori_loop(0, 4, out_grads, 0)
-    o_core = send(r.w_o.at[(*whole, other)], r.core_o, "c", "o_core")
-    reduce_add("w", 2, back_w[2])
-    start(back_w[1])
-    flush()
-
-    def part_da(blk):
-        acc = dot_nt(r.dgu[0, blk, :, 0:QKV], w_qkv(0)) + dot_nt(r.dgu[1, blk, :, 0:QKV], w_qkv(1))
-        r.gains[0:1] += jnp.sum(acc * r.a_full[blk].astype(F32), axis=0, keepdims=True)
-        return acc
-
-    back_o = {step: reduce_later("o", step) for step in range(4)}
-    back_q = {step: reduce_later("q", step) for step in range(4)}
-
-    def tail_q():
-        core_sum("q", r.core_q, q_core)
-        start(back_q[3])
-
-    def tail_o():
-        core_sum("o", r.core_o, o_core)
-        start(back_o[3])
-
-    a_relay, a_finish = square_sum(part_da, {1: tail_q, 3: tail_o})
-
-    gain_links = ["c", "za", "zb", "yo", "xo", "y", "x"]
-
-    def gain_send(n):
-        return send(r.gains, r.gain_in.at[n], gain_links[n], ("gain", n))
-
-    def gain_add(n, copy):
-        copy.wait_send()
-        copy.wait_recv()
-        r.gains[...] += r.gain_in[n]
-
     sum_pair = r.w_m.at[own_slot]
     back_x = later(sum_pair, r.mlp_x, "x", "mlp_x", gives=lends == 1, takes=lends == 0)
     back_y0 = later(r.mlp_x, r.raw.at[0], "y", "raw_y", gives=role == 0, takes=role == 0)
     back_y1 = later(sum_pair, r.raw.at[0], "y", "raw_y", gives=role == 1, takes=role == 1)
     mlp_back_c = later(r.mlp_sum.at[flip(core)], r.mlp_c, "c", "raw_c0", gives=lends == 0, takes=lends == 1)
 
+    lax.fori_loop(0, 4, qkv_grads, 0)
+    flush()
+    q_core = send(r.m_full.at[(*whole, other)], r.core_q, "c", "q_core")
+
+    def part_da(blk):
+        acc = dot_nt(r.dgu[0, blk, :, 0:QKV], w_qkv(0)) + dot_nt(r.dgu[1, blk, :, 0:QKV], w_qkv(1))
+        r.gains[0:1] += jnp.sum(acc * r.a_full[blk].astype(F32), axis=0, keepdims=True)
+        return acc
+
+    back_o = {step: reduce_later("o", step) for step in range(4)}
+    back_q = {step: reduce_later("q", step) for step in range(4)}
+
+    def tail_q():
+        core_sum("q", r.core_q, q_core)
+        start(back_q[3])
+
+    def tail_o():
+        core_sum("o", r.core_o, o_core)
+        start(back_o[3])
+
+    a_relay, a_finish = square_sum(part_da, {0: tail_o, 1: tail_q})
+
+    gain_links = ["c", "za", "zb", "yo", "xo", "y", "x"]
+
+    def gain_send(n):
+        return send(r.gains, r.gain_in.at[n], gain_links[n], ("gain", n))
+
+    def gain_add(n, copy):
+        copy.wait_send()
+        copy.wait_recv()
+        r.gains[...] += r.gain_in[n]
+
     def reduce_next(kind, step, back):
         reduce_add(kind, step, back[step])
         start(back[step - 1])
@@ -838,25 +845,23 @@
     reduce_next("w", 1, back_w)
     gain_add(0, g_step)
     g_step = gain_send(1)
+    reduce_next("o", 3, back_o)
+    a_relay()
     reduce_next("q", 3, back_q)
-    a_relay()
-    reduce_next("o", 3, back_o)
     gain_add(1, g_step)
     g_step = gain_send(2)
     reduce_add("w", 0, back_w[0])
     back_x.start()
     back_y1.start()
+    reduce_next("o", 2, back_o)
     r.layer_out[...] = reorder(down_finish()).astype(BF16)
-    reduce_next("q", 2, back_q)
-    reduce_next("o", 2, back_o)
     gain_add(2, g_step)
     g_step = gain_send(3)
-    back_x.wait_recv()
-    back_y0.start()
-    reduce_next("q", 1, back_q)
+    reduce_next("q", 2, back_q)
     reduce_next("o", 1, back_o)
     gain_add(3, g_step)
     g_step = gain_send(4)
+    reduce_next("q", 1, back_q)
 
     def last_step(kind, group, cols):
         for part in range(4):
@@ -867,16 +872,17 @@
         r.attn_low[:, cols] = r.attn_sum[:, cols].astype(BF16)
 
     last_step("o", back_o[0], slice(QKV, AW))
-    last_step("q", back_q[0], slice(0, QKV))
-    attn_back = send(r.attn_low, r.attn_x, "x", "swap_q", gives=odd, takes=odd)
-    gain_add(4, g_step)
-    g_step = gain_send(5)
-
     rows_x = rows_in()
     inv_a = row_scale(rows_x)
     scaled = a_finish() * attn_gain
     inner = jnp.mean(scaled * rows_x, axis=-1, keepdims=True)
     r.input_grad[...] = reorder(r.resid[...] + inv_a * scaled - rows_x * (inv_a * inv_a * inv_a * inner))
+    gain_add(4, g_step)
+    g_step = gain_send(5)
+    last_step("q", back_q[0], slice(0, QKV))
+    attn_back = send(r.attn_low, r.attn_x, "x", "swap_q", gives=odd, takes=odd)
+    back_x.wait_recv()
+    back_y0.start()
     gain_add(5, g_step)
     g_step = gain_send(6)
     back_y0.wait_recv()

time: 160 us -> 156 us (0.975); the launches traced: 160 us -> 154 us
  Pallas kernels: 159 us -> 153 us
    pallas_call x1, Pallas kernels: 157 us -> 151 us  [body(): pl.pallas_call(kernel, out_shape=(jax.ShapeDtypeStruct((ROWS, WIDTH), BF1...]
where the time goes in v4:
time: 156 us; the launch traced here: 154 us
  Pallas kernels  153 us (98%)
    pallas_call x1, Pallas kernels, body(): pl.pallas_call(kernel, out_shape=(jax.ShapeDtypeStruct((ROWS, WIDTH), BF1...  151 us

profile of v4, /device:TPU:8, one launch (start us, length us, event | category | flops | bytes accessed | tf_op | source)
XLA Modules:
  0.0 154.2 jit_solution(960290505580589983)
XLA Ops:
  0.6 150.5 %layer.1 = (bf16[256,1024]{1,0:T(8,128)(2,1)}, f32[256,1024]{1,0:T(8,128)}, f32[64,768]{1,0:T(8,128)}, f32[64,1152]{1,0:T(8,128)}, f32[8,1024]{1,0:T(8,128)}) custom-call(bf16[256,1024]{1,0:T(8,128)(2,1)} %refs_0_.1, bf16[256,1024]{1,0:T(8,128)(2,1)} %refs_1_.1, bf16[64,256]{1,0:T(8,128)(2,1)} %refs_2_.1, bf16[64,128]{1,0:T(8,128)(2,1)} %refs_3_.1, ...), custom_call_target="tpu_custom_call" | custom-call | tf_op jit(solution)/shard_map/layer/pallas_call | solution.py:991
  151.2 2.9 %unpack.1 = (bf16[256,1024]{1,0:T(8,128)(2,1)}, f32[256,1024]{1,0:T(8,128)}, f32[1024]{0:T(1024)}, f32[64,256]{1,0:T(8,128)}, f32[64,128]{1,0:T(8,128)}, /*index...) custom-call(bf16[256,1024]{1,0:T(8,128)(2,1)} %get-tuple-element.31., ...), custom_call_target="tpu_custom_call" | custom-call | tf_op jit(solution)/shard_map/unpack/pallas_call | solution.py:1024

commit v5 on v4

--- a/solution.py
+++ b/solution.py
@@ -558,6 +558,8 @@
 
     o_relay, o_finish = square_sum(attend_and_part, {3: lambda: advance("w", 3)})
     o_relay()
+    r.dk[...] = jnp.zeros((2, 4, ROWS, HEAD), F32)
+    r.dv[...] = jnp.zeros((2, 4, ROWS, HEAD), F32)
     c_pair.wait_recv()
     c_forward = send(r.c_full.at[core + 2], r.c_full.at[core + 2], "c", "cot_f")
     resid = rows_in() + o_finish()
@@ -684,11 +686,12 @@
     r.resid[...] = dresid
     r.d_full[square(0)] = dresid.astype(BF16)
     d_second, d_forward, d_x1, d_y0, d_far = square_gather(r.d_full)
+    def down_order(n):
+        return jnp.where(n == 0, 2, jnp.where(n == 3, 3, n - 1))
+
     down_block, down_finish, down_pair = pair_sum(part_down, r.sum_d, r.input_grad, "down", True)
-    lax.fori_loop(0, 4, down_block, 0)
+    lax.fori_loop(0, 4, lambda n, carry: down_block(down_order(n), carry), 0)
     d_second()
-    r.dk[...] = jnp.zeros((2, 4, ROWS, HEAD), F32)
-    r.dv[...] = jnp.zeros((2, 4, ROWS, HEAD), F32)
 
     def back_step(i, j, carry, diagonal, delta):
         out = []
@@ -776,8 +779,7 @@
 
     reduce_add("w", 2, back_w[2])
     start(back_w[1])
-    lax.fori_loop(0, 4, out_grads, 0)
-    o_core = send(r.w_o.at[(*whole, other)], r.core_o, "c", "o_core")
+
     def key_block(j, gain_sum):
         for g in range(2):
             grad = turn_back(r.dk[g, j] * SCORE_SCALE, j)
@@ -808,6 +810,8 @@
     lax.fori_loop(0, 4, qkv_grads, 0)
     flush()
     q_core = send(r.m_full.at[(*whole, other)], r.core_q, "c", "q_core")
+    lax.fori_loop(0, 4, out_grads, 0)
+    o_core = send(r.w_o.at[(*whole, other)], r.core_o, "c", "o_core")
 
     def part_da(blk):
         acc = dot_nt(r.dgu[0, blk, :, 0:QKV], w_qkv(0)) + dot_nt(r.dgu[1, blk, :, 0:QKV], w_qkv(1))
@@ -825,7 +829,7 @@
         core_sum("o", r.core_o, o_core)
         start(back_o[3])
 
-    a_relay, a_finish = square_sum(part_da, {0: tail_o, 1: tail_q})
+    a_relay, a_finish = square_sum(part_da, {1: tail_q, 3: tail_o})
 
     gain_links = ["c", "za", "zb", "yo", "xo", "y", "x"]
 
@@ -845,23 +849,23 @@
     reduce_next("w", 1, back_w)
     gain_add(0, g_step)
     g_step = gain_send(1)
-    reduce_next("o", 3, back_o)
     a_relay()
     reduce_next("q", 3, back_q)
+    reduce_next("o", 3, back_o)
     gain_add(1, g_step)
     g_step = gain_send(2)
     reduce_add("w", 0, back_w[0])
     back_x.start()
     back_y1.start()
-    reduce_next("o", 2, back_o)
     r.layer_out[...] = reorder(down_finish()).astype(BF16)
     gain_add(2, g_step)
     g_step = gain_send(3)
     reduce_next("q", 2, back_q)
-    reduce_next("o", 1, back_o)
+    reduce_next("o", 2, back_o)
     gain_add(3, g_step)
     g_step = gain_send(4)
     reduce_next("q", 1, back_q)
+    reduce_next("o", 1, back_o)
 
     def last_step(kind, group, cols):
         for part in range(4):
@@ -871,18 +875,18 @@
             r.attn_sum[16 * part : 16 * part + 16, cols] = total.reshape(16, -1)
         r.attn_low[:, cols] = r.attn_sum[:, cols].astype(BF16)
 
+    back_x.wait_recv()
+    back_y0.start()
+    gain_add(4, g_step)
+    g_step = gain_send(5)
+    last_step("q", back_q[0], slice(0, QKV))
     last_step("o", back_o[0], slice(QKV, AW))
+    attn_back = send(r.attn_low, r.attn_x, "x", "swap_q", gives=odd, takes=odd)
     rows_x = rows_in()
     inv_a = row_scale(rows_x)
     scaled = a_finish() * attn_gain
     inner = jnp.mean(scaled * rows_x, axis=-1, keepdims=True)
     r.input_grad[...] = reorder(r.resid[...] + inv_a * scaled - rows_x * (inv_a * inv_a * inv_a * inner))
-    gain_add(4, g_step)
-    g_step = gain_send(5)
-    last_step("q", back_q[0], slice(0, QKV))
-    attn_back = send(r.attn_low, r.attn_x, "x", "swap_q", gives=odd, takes=odd)
-    back_x.wait_recv()
-    back_y0.start()
     gain_add(5, g_step)
     g_step = gain_send(6)
     back_y0.wait_recv()

time: 156 us -> 156 us (level)
  no operation moved by 1% of the time
where the time goes in v5:
time: 156 us; the launch traced here: 153 us
  Pallas kernels  152 us (97%)
    pallas_call x1, Pallas kernels, body(): pl.pallas_call(kernel, out_shape=(jax.ShapeDtypeStruct((ROWS, WIDTH), BF1...  150 us

profile of v5, /device:TPU:8, one launch (start us, length us, event | category | flops | bytes accessed | tf_op | source)
XLA Modules:
  0.0 153.2 jit_solution(7907637912434780410)
XLA Ops:
  0.6 149.5 %layer.1 = (bf16[256,1024]{1,0:T(8,128)(2,1)}, f32[256,1024]{1,0:T(8,128)}, f32[64,768]{1,0:T(8,128)}, f32[64,1152]{1,0:T(8,128)}, f32[8,1024]{1,0:T(8,128)}) custom-call(bf16[256,1024]{1,0:T(8,128)(2,1)} %refs_0_.1, bf16[256,1024]{1,0:T(8,128)(2,1)} %refs_1_.1, bf16[64,256]{1,0:T(8,128)(2,1)} %refs_2_.1, bf16[64,128]{1,0:T(8,128)(2,1)} %refs_3_.1, ...), custom_call_target="tpu_custom_call" | custom-call | tf_op jit(solution)/shard_map/layer/pallas_call | solution.py:995
  150.2 2.9 %unpack.1 = (bf16[256,1024]{1,0:T(8,128)(2,1)}, f32[256,1024]{1,0:T(8,128)}, f32[1024]{0:T(1024)}, f32[64,256]{1,0:T(8,128)}, f32[64,128]{1,0:T(8,128)}, /*index...) custom-call(bf16[256,1024]{1,0:T(8,128)(2,1)} %get-tuple-element.31., ...), custom_call_target="tpu_custom_call" | custom-call | tf_op jit(solution)/shard_map/unpack/pallas_call | solution.py:1028

commit v6 on v5

--- a/solution.py
+++ b/solution.py
@@ -810,8 +810,6 @@
     lax.fori_loop(0, 4, qkv_grads, 0)
     flush()
     q_core = send(r.m_full.at[(*whole, other)], r.core_q, "c", "q_core")
-    lax.fori_loop(0, 4, out_grads, 0)
-    o_core = send(r.w_o.at[(*whole, other)], r.core_o, "c", "o_core")
 
     def part_da(blk):
         acc = dot_nt(r.dgu[0, blk, :, 0:QKV], w_qkv(0)) + dot_nt(r.dgu[1, blk, :, 0:QKV], w_qkv(1))
@@ -825,11 +823,9 @@
         core_sum("q", r.core_q, q_core)
         start(back_q[3])
 
-    def tail_o():
-        core_sum("o", r.core_o, o_core)
-        start(back_o[3])
-
-    a_relay, a_finish = square_sum(part_da, {1: tail_q, 3: tail_o})
+    a_relay, a_finish = square_sum(part_da, {3: tail_q})
+    lax.fori_loop(0, 4, out_grads, 0)
+    o_core = send(r.w_o.at[(*whole, other)], r.core_o, "c", "o_core")
 
     gain_links = ["c", "za", "zb", "yo", "xo", "y", "x"]
 
@@ -849,6 +845,8 @@
     reduce_next("w", 1, back_w)
     gain_add(0, g_step)
     g_step = gain_send(1)
+    core_sum("o", r.core_o, o_core)
+    start(back_o[3])
     a_relay()
     reduce_next("q", 3, back_q)
     reduce_next("o", 3, back_o)

time: 156 us -> 153 us (0.981); the launches traced: 153 us -> 152 us
  no operation moved by 1% of the time
where the time goes in v6:
time: 153 us; the launch traced here: 152 us
  Pallas kernels  151 us (99%)
    pallas_call x1, Pallas kernels, body(): pl.pallas_call(kernel, out_shape=(jax.ShapeDtypeStruct((ROWS, WIDTH), BF1...  148 us

profile of v6, /device:TPU:8, one launch (start us, length us, event | category | flops | bytes accessed | tf_op | source)
XLA Modules:
  0.0 151.8 jit_solution(13015782441992198825)
XLA Ops:
  0.6 148.1 %layer.1 = (bf16[256,1024]{1,0:T(8,128)(2,1)}, f32[256,1024]{1,0:T(8,128)}, f32[64,768]{1,0:T(8,128)}, f32[64,1152]{1,0:T(8,128)}, f32[8,1024]{1,0:T(8,128)}) custom-call(bf16[256,1024]{1,0:T(8,128)(2,1)} %refs_0_.1, bf16[256,1024]{1,0:T(8,128)(2,1)} %refs_1_.1, bf16[64,256]{1,0:T(8,128)(2,1)} %refs_2_.1, bf16[64,128]{1,0:T(8,128)(2,1)} %refs_3_.1, ...), custom_call_target="tpu_custom_call" | custom-call | tf_op jit(solution)/shard_map/layer/pallas_call | solution.py:993
  148.8 2.9 %unpack.1 = (bf16[256,1024]{1,0:T(8,128)(2,1)}, f32[256,1024]{1,0:T(8,128)}, f32[1024]{0:T(1024)}, f32[64,256]{1,0:T(8,128)}, f32[64,128]{1,0:T(8,128)}, /*index...) custom-call(bf16[256,1024]{1,0:T(8,128)(2,1)} %get-tuple-element.31., ...), custom_call_target="tpu_custom_call" | custom-call | tf_op jit(solution)/shard_map/unpack/pallas_call | solution.py:1026
